TPU v7x, 128 devices: a whole 4x4x4 slice. The times are simulated.
128 devices in a mesh: bx: 8 (over y, core), by: 16 (over z, x).
Axes of the slice: x: 4, y: 4, z: 4, core: 2. Of those that a mesh axis runs over, the one named last changes fastest.
Arguments:
- features: bfloat16 [256, 8, 8, 8, 128], P(('bx', 'by')), may hold values from -6 to 6
- weight: bfloat16 [27, 128, 128], replicated, may hold values from -0.109375 to 0.109375
- down_weight: bfloat16 [8, 128, 128], replicated, may hold values from -0.1875 to 0.1875
- grad_out: bfloat16 [256, 8, 8, 8, 128], P(('bx', 'by')), may hold values from -6 to 6
- grad_coarse: bfloat16 [256, 64, 128], P(('bx', 'by')), may hold values from -6 to 6
- neighbours: int32 [256, 27], P(('bx', 'by')), may hold values from 0 to 20, as said below
- send_list: int32 [1152, 2], P(('bx', 'by')), may hold values from -1 to 1, as said below
- coarse_dest: int32 [256], P(('bx', 'by')), may hold values from 0 to 15, as said below
- coarse_from: int32 [256], P(('bx', 'by')), may hold values from 0 to 15, as said below
Outputs:
- hidden: bfloat16 [256, 8, 8, 8, 128], P(('bx', 'by'))
- coarse: bfloat16 [256, 64, 128], P(('bx', 'by'))
- grad_features: bfloat16 [256, 8, 8, 8, 128], P(('bx', 'by'))
- grad_weight: float32 [27, 128, 128], replicated
- grad_down: float32 [8, 128, 128], replicated
Inputs may be any that keep to these rules, and one draw needn't show every extreme that they name: `neighbours`: entry 13 of a row is the block's own slot. Values under 2 are blocks of the same device; values 2 + 2 e + j name the j-th block that the device at bx offset e div 3 - 1 and by offset e mod 3 - 1 lists toward this device; the value 2 + 9 * 2 means no neighbour. Neighbourhood is symmetric. `send_list`: row 9 d + e lists, in rising order and then -1, exactly the slots of device d that are neighbours of some block of the device at bx offset e div 3 - 1, by offset e mod 3 - 1; row e = 4 is all -1. Some device fills all 2 slots of a row. Slot s of a device goes to coarse slot s of the device in the same bx row with by index coarse_dest; one device sends at most 1 block to one owner, and every device sends exactly 1 to some owner. `coarse_from`: coarse slot m of a device holds slot m of the device in the same bx row with this by index; together with coarse_dest each block reaches exactly one coarse slot.
All inputs are finite; a program needn't handle non-finite values.
Results may differ from a plain program's by a relative error of at most 0.0049.
Values may be sent and summed in bfloat16 or wider, within the bound.
A program may use at most 128 MiB of HBM per device.

v0:
```python
import functools

import jax
import jax.numpy as jnp
from jax import lax
from jax.experimental import pallas as pl
from jax.experimental.pallas import tpu as pltpu
from jax.sharding import PartitionSpec as P

OFFSETS = [(p, q, w) for p in (-1, 0, 1) for q in (-1, 0, 1) for w in (-1, 0, 1)]


def with_halo(cells, sides, width):
    for axis, dim in sides:
        count = lax.axis_size(axis)
        ends = count - 1
        head = lax.slice_in_dim(cells, 0, width, axis=dim)
        tail = lax.slice_in_dim(cells, cells.shape[dim] - width, cells.shape[dim], axis=dim)
        cells = jnp.concatenate(
            [
                lax.ppermute(tail, axis, [(i, (i + 1) % count) for i in range(ends)]),
                cells,
                lax.ppermute(head, axis, [((i + 1) % count, i) for i in range(ends)]),
            ],
            axis=dim,
        )
    return cells


def offset_index(offset):
    return (offset[0] + 1) * 9 + (offset[1] + 1) * 3 + offset[2] + 1


def span_of(step, edge_len):
    if step == -1:
        return slice(edge_len - 1, edge_len)
    if step == 1:
        return slice(0, 1)
    return slice(0, edge_len)


def assemble(piece_at):
    planes = []
    for step_x in (-1, 0, 1):
        lines = []
        for step_y in (-1, 0, 1):
            cells = [piece_at((step_x, step_y, step_z)) for step_z in (-1, 0, 1)]
            lines.append(jnp.concatenate(cells, axis=3))
        planes.append(jnp.concatenate(lines, axis=2))
    return jnp.concatenate(planes, axis=1)


def window(padded, offset, sign):
    edge_len = padded.shape[1] - 2
    starts = [1 + sign * offset[axis_id] for axis_id in range(3)]
    return padded[
        :,
        starts[0] : starts[0] + edge_len,
        starts[1] : starts[1] + edge_len,
        starts[2] : starts[2] + edge_len,
    ]


def conv_rows(padded, weight, sign):
    channels = padded.shape[-1]
    running = None
    for offset in OFFSETS:
        shifted = window(padded, offset, sign).reshape(-1, channels)
        matrix = weight[offset_index(offset)]
        if sign < 0:
            matrix = matrix.T
        term = jnp.dot(shifted, matrix, preferred_element_type=jnp.float32)
        running = term if running is None else running + term
    return running


def contract(left, right):
    return lax.dot_general(
        left, right, (((0,), (0,)), ((), ())), preferred_element_type=jnp.float32
    )


def children(hidden):
    block_count, edge_len, channels = (hidden.shape[0], hidden.shape[1], hidden.shape[-1])
    half_edge = edge_len // 2
    parted = hidden.reshape(block_count, half_edge, 2, half_edge, 2, half_edge, 2, channels)
    return [
        parted[:, :, i, :, j, :, l, :].reshape(-1, channels)
        for i in (0, 1)
        for j in (0, 1)
        for l in (0, 1)
    ]


def down_blocks(hidden, down_weight):
    block_count, channels = (hidden.shape[0], hidden.shape[-1])
    running = None
    for child_id, rows_in in enumerate(children(hidden)):
        term = jnp.dot(rows_in, down_weight[child_id], preferred_element_type=jnp.float32)
        running = term if running is None else running + term
    return running.reshape(block_count, -1, channels)


def up_blocks(coarse_grad, down_weight, edge_len):
    block_count, channels = (coarse_grad.shape[0], coarse_grad.shape[-1])
    half_edge = edge_len // 2
    flat_grad = coarse_grad.reshape(-1, channels)
    parts_list = [
        jnp.dot(flat_grad, down_weight[child_id].T, preferred_element_type=jnp.float32)
        for child_id in range(8)
    ]
    stacked = jnp.stack(parts_list).reshape(
        2, 2, 2, block_count, half_edge, half_edge, half_edge, channels
    )
    return stacked.transpose(3, 4, 0, 5, 1, 6, 2, 7).reshape(
        block_count, edge_len, edge_len, edge_len, channels
    )


def face_stack(blocks):
    return jnp.stack(
        [
            blocks[:, 0],
            blocks[:, -1],
            blocks[:, :, 0],
            blocks[:, :, -1],
            blocks[:, :, :, 0],
            blocks[:, :, :, -1],
        ],
        axis=1,
    )


def listed_faces(blocks, send_list):
    block_count = blocks.shape[0]
    all_faces = face_stack(blocks)
    zero_face = jnp.zeros((1,) + all_faces.shape[1:], all_faces.dtype)
    extended = jnp.concatenate([all_faces, zero_face], axis=0)
    picked = jnp.take(extended, jnp.where(send_list < 0, block_count, send_list), axis=0)
    return (all_faces, zero_face, picked)


def build_padded(blocks, face_pool, neighbours):
    edge_len = blocks.shape[1]

    def piece_at(offset):
        if offset == (0, 0, 0):
            return blocks
        axis_lead = [axis_id for axis_id in range(3) if offset[axis_id] != 0][0]
        face_id = 2 * axis_lead + (0 if offset[axis_lead] == 1 else 1)
        face_rows = jnp.take(face_pool, neighbours[:, offset_index(offset)] * 6 + face_id, axis=0)
        others = [axis_id for axis_id in range(3) if axis_id != axis_lead]
        face_rows = face_rows[
            :, span_of(offset[others[0]], edge_len), span_of(offset[others[1]], edge_len)
        ]
        return jnp.expand_dims(face_rows, 1 + axis_lead)

    return assemble(piece_at)


def padded_for(blocks, send_list, neighbours):
    slot_cap = send_list.shape[1]
    all_faces, zero_face, picked = listed_faces(blocks, send_list)
    outgoing = picked.reshape((3, 3) + picked.shape[1:])
    padded = with_halo(outgoing, (("bx", 0), ("by", 1)), 1)
    received = padded[::2, ::2]
    face_pool = jnp.concatenate(
        [all_faces, received.reshape((9 * slot_cap,) + all_faces.shape[1:]), zero_face], axis=0
    )
    return build_padded(blocks, face_pool.reshape((-1,) + all_faces.shape[2:]), neighbours)


def prior_count(owners, columns):
    onehot = (owners[:, None] == jnp.arange(columns, dtype=jnp.int32)[None, :]).astype(jnp.int32)
    before = jnp.cumsum(onehot, axis=0) - onehot
    return jnp.sum(before * onehot, axis=1)


def general_path(
    features,
    weight,
    down_weight,
    grad_out,
    grad_coarse,
    neighbours,
    send_list,
    coarse_dest,
    coarse_from,
):
    block_count, edge_len, channels = (features.shape[0], features.shape[1], features.shape[-1])
    device_total = lax.axis_size("bx") * lax.axis_size("by")
    padded_in = padded_for(features, send_list, neighbours)
    preact = conv_rows(padded_in, weight, 1).reshape(features.shape)
    hidden = jax.nn.silu(preact).astype(jnp.bfloat16)
    reduced = down_blocks(hidden, down_weight).astype(jnp.bfloat16)
    columns = lax.axis_size("by")
    per_peer = -(-block_count // columns)
    send_rank = prior_count(coarse_dest, columns)
    recv_rank = prior_count(coarse_from, columns)
    outgoing = jnp.zeros((columns * per_peer,) + reduced.shape[1:], jnp.bfloat16)
    outgoing = outgoing.at[coarse_dest * per_peer + send_rank].set(reduced)
    arrived = lax.all_to_all(outgoing, "by", split_axis=0, concat_axis=0, tiled=True)
    coarse = arrived[coarse_from * per_peer + recv_rank]
    returning = jnp.zeros((columns * per_peer,) + grad_coarse.shape[1:], jnp.bfloat16)
    returning = returning.at[coarse_from * per_peer + recv_rank].set(grad_coarse)
    came_back = lax.all_to_all(returning, "by", split_axis=0, concat_axis=0, tiled=True)
    coarse_grad_here = came_back[coarse_dest * per_peer + send_rank]
    flat_grad = coarse_grad_here.reshape(-1, channels)
    down_terms = jnp.stack([contract(rows_in, flat_grad) for rows_in in children(hidden)])
    sigmoid_pre = jax.nn.sigmoid(preact)
    grad_pre = (
        (grad_out.astype(jnp.float32) + up_blocks(coarse_grad_here, down_weight, edge_len))
        * sigmoid_pre
        * (1.0 + preact * (1.0 - sigmoid_pre))
    ).astype(jnp.bfloat16)
    padded_grad = padded_for(grad_pre, send_list, neighbours)
    grad_features = conv_rows(padded_grad, weight, -1).reshape(features.shape).astype(jnp.bfloat16)
    own_rows = grad_pre.reshape(-1, channels)
    weight_terms = jnp.stack(
        [
            contract(window(padded_in, offset, 1).reshape(-1, channels), own_rows)
            for offset in OFFSETS
        ]
    )
    weight_total, down_total = lax.psum((weight_terms, down_terms), ("bx", "by"))
    return (hidden, coarse, grad_features, weight_total / device_total, down_total / device_total)


F32, BF16 = jnp.float32, jnp.bfloat16
MESH = pl.DeviceIdType.MESH
NONE = 20
LISTS = 9
ROUTES = (("x", "y", "z"), ("y", "z", "x"), ("z", "x", "y"))
PART_ROWS = 1536
HALF_ROWS = 768


def fits_grid(p, o1, o2):
    half = p // 2
    good = (half == 0) | (half == NONE // 2)
    for dr in {0, o1}:
        for dc in {0, o2}:
            if (dr, dc) != (0, 0):
                good = good | (half == (dr + 1) * 3 + dc + 2)
    return good


def section_kernel(
    sizes,
    nb, sl, cdest, cfrom,
    feat, weight, down, gout, gcoarse,
    hid_out, coarse_out, gfeat_out, gw_out, gd_out, flag_out,
    pad, col, colg, xpool, ypool, cpool,
    xs, ys, cs, xr, yr, cr,
    gsend, gpool, rsend, rpool,
    wback, wdcat, slope, hpart, wide, cgx, up, gbf,
    arf, s0, r0, hf, s1, r1, t1f, s2, r2, r3, fin,
    halo_send, halo_recv, g_send, g_recv, c_send, c_recv, ar_send, ar_recv, core_send, core_recv,
):
    nx, ny, nz = sizes
    nby, nbx = nx * nz, 2 * ny
    r, c = lax.axis_index("bx"), lax.axis_index("by")
    core, at = lax.rem(r, 2), {"x": lax.rem(c, nx), "y": r // 2, "z": c // nx}
    size = {"x": nx, "y": ny, "z": nz}

    def moved(axis, step):
        to = dict(at)
        to[axis] = lax.rem(at[axis] + step, size[axis])
        return (to["y"] * 2 + core, to["z"] * nx + to["x"])

    other_core = (r + 1 - 2 * core, c)

    def beside(dr, dc):
        return (lax.rem(r + dr + nbx, nbx), lax.rem(c + dc + nby, nby))

    around = [(dr, dc) for dr in (-1, 0, 1) for dc in (-1, 0, 1) if (dr, dc) != (0, 0)]

    barrier = pltpu.get_barrier_semaphore()

    def greet(step, carry):
        pl.semaphore_signal(barrier, inc=1, device_id=(r, lax.rem(c + step, nby)), device_id_type=MESH)
        return carry

    lax.fori_loop(1, nby, greet, 0)
    met = nby - 1
    for dr, dc in around:
        if dr != 0:
            pl.semaphore_signal(barrier, inc=1, device_id=beside(dr, dc), device_id_type=MESH)
            met += 1
    for step in range(1, ny):
        pl.semaphore_signal(barrier, inc=1, device_id=moved("y", step), device_id_type=MESH)
        met += 1

    def fill_interior(i, carry):
        b, x = i // 8, lax.rem(i, 8)
        pad[b, x + 1, 1:9, 1:9, :] = feat[b, x].astype(F32).reshape(8, 8, 128)
        return carry

    lax.fori_loop(0, 16, fill_interior, 0)
    pad[2, 1:9, 1:9] = jnp.zeros((8, 8, 16, 128), F32)
    for side in (0, 1):
        xpool[side, NONE] = jnp.zeros((8, 8, 128), F32)
        ypool[side, NONE] = jnp.zeros((8, 8, 128), F32)
    for corner in range(4):
        cpool[corner, NONE] = jnp.zeros((8, 128), F32)

    near = (8, 1)
    edge = (1, 8)

    def stage_faces(t):
        for side in (0, 1):
            step = 2 * side - 1
            for j in (0, 1):
                bx_block = jnp.maximum(sl[(step + 1) * 3 + 1, j], 0)
                face = pad[bx_block, edge[side], 1:9, 1:9, :]
                xs[t, side, 64 * j : 64 * j + 64] = face.reshape(64, 128).astype(BF16)
                by_block = jnp.maximum(sl[3 + step + 1, j], 0)
                face = pad[by_block, 1:9, edge[side], 1:9, :]
                ys[t, side, 64 * j : 64 * j + 64] = face.reshape(64, 128).astype(BF16)
        for sx in (0, 1):
            for sy in (0, 1):
                row = 2 * sx * 3 + 2 * sy
                lines = [pad[jnp.maximum(sl[row, j], 0), edge[sx], edge[sy], 1:9, :] for j in (0, 1)]
                cs[t, 2 * sx + sy] = jnp.concatenate(lines, axis=0).astype(BF16)

    def halo_copies(t):
        out = []
        for side in (0, 1):
            out.append((xs.at[t, side], xr.at[t, 1 - side], beside(2 * side - 1, 0)))
        for side in (0, 1):
            out.append((ys.at[t, side], yr.at[t, 1 - side], beside(0, 2 * side - 1)))
        for sx in (0, 1):
            for sy in (0, 1):
                out.append((cs.at[t, 2 * sx + sy], cr.at[t, 3 - 2 * sx - sy], beside(2 * sx - 1, 2 * sy - 1)))
        return [
            pltpu.make_async_remote_copy(
                src_ref=src, dst_ref=dst, send_sem=halo_send.at[t, n], recv_sem=halo_recv.at[t, n],
                device_id=to, device_id_type=MESH,
            )
            for n, (src, dst, to) in enumerate(out)
        ]

    def local_pools():
        for side in (0, 1):
            for b in (0, 1):
                xpool[side, b] = pad[b, near[side], 1:9, 1:9, :]
                ypool[side, b] = pad[b, 1:9, near[side], 1:9, :]
        for sx in (0, 1):
            for sy in (0, 1):
                for b in (0, 1):
                    cpool[2 * sx + sy, b] = pad[b, near[sx], near[sy], 1:9, :]

    def remote_pools(t):
        for side in (0, 1):
            for j in (0, 1):
                ex, ey = 2 * side * 3 + 1, 3 + 2 * side
                xpool[side, 2 + 2 * ex + j] = xr[t, side, 64 * j : 64 * j + 64].astype(F32).reshape(8, 8, 128)
                ypool[side, 2 + 2 * ey + j] = yr[t, side, 64 * j : 64 * j + 64].astype(F32).reshape(8, 8, 128)
        for sx in (0, 1):
            for sy in (0, 1):
                lines = cr[t, 2 * sx + sy].astype(F32).reshape(2, 8, 128)
                for j in (0, 1):
                    ex, ey, ec = 2 * sx * 3 + 1, 3 + 2 * sy, 2 * sx * 3 + 2 * sy
                    cpool[2 * sx + sy, 2 + 2 * ex + j] = xpool[sx, 2 + 2 * ex + j, near[sy] - 1]
                    cpool[2 * sx + sy, 2 + 2 * ey + j] = ypool[sy, 2 + 2 * ey + j, near[sx] - 1]
                    cpool[2 * sx + sy, 2 + 2 * ec + j] = lines[j]

    def rims():
        def one(b, carry):
            for o1 in (-1, 0, 1):
                for o2 in (-1, 0, 1):
                    for o3 in (-1, 0, 1):
                        if (o1, o2, o3) == (0, 0, 0):
                            continue
                        p = nb[b, offset_index((o1, o2, o3))]
                        x, y, z = [(0, None, 9)[o + 1] for o in (o1, o2, o3)]
                        zs = (8, None, 1)[o3 + 1]
                        if o1 == 0 and o2 == 0:
                            pad[b, 1:9, 1:9, z : z + 1, :] = pad[jnp.minimum(p, 2), 1:9, 1:9, zs : zs + 1, :]
                        elif o2 == 0:
                            s = (o1 + 1) // 2
                            if o3 == 0:
                                pad[b, x, 1:9, 1:9, :] = xpool[s, p]
                            else:
                                pad[b, x, 1:9, z : z + 1, :] = xpool[s, p, :, zs - 1 : zs, :]
                        elif o1 == 0:
                            s = (o2 + 1) // 2
                            if o3 == 0:
                                pad[b, 1:9, y, 1:9, :] = ypool[s, p]
                            else:
                                pad[b, 1:9, y, z : z + 1, :] = ypool[s, p, :, zs - 1 : zs, :]
                        else:
                            s = (o1 + 1) + (o2 + 1) // 2
                            if o3 == 0:
                                pad[b, x, y, 1:9, :] = cpool[s, p]
                            else:
                                pad[b, x, y, z : z + 1, :] = cpool[s, p, zs - 1 : zs, :]
            return carry

        lax.fori_loop(0, 2, one, 0)

    def columns(dst):
        def one(i, carry):
            b, x = i // 10, lax.rem(i, 10)
            for m in range(9):
                o2, o3 = m // 3, m % 3
                cells = pad[b, x, o2 : o2 + 8, o3 : o3 + 8, :]
                dst[i, :, 128 * m : 128 * m + 128] = cells.reshape(64, 128).astype(BF16)
            return carry

        lax.fori_loop(0, 20, one, 0)

    stage_faces(0)

    def stage_gcoarse(step, carry):
        to = lax.rem(c + step, nby)
        gsend[step] = gcoarse[jnp.where(cfrom[1] == to, 1, 0)]
        return carry

    lax.fori_loop(0, nby, stage_gcoarse, 0)
    gpool[0] = gsend[0]

    pl.semaphore_wait(barrier, met)
    first = halo_copies(0)
    for copy in first:
        copy.start()

    def row_copy(src, dst, send, recv, step):
        return pltpu.make_async_remote_copy(
            src_ref=src.at[step], dst_ref=dst.at[step], send_sem=send.at[step], recv_sem=recv.at[step],
            device_id=(r, lax.rem(c + step, nby)), device_id_type=MESH,
        )

    def start_row(src, dst, send, recv):
        def one(step, carry):
            row_copy(src, dst, send, recv, step).start()
            return carry

        lax.fori_loop(1, nby, one, 0)

    def wait_row_recv(src, dst, send, recv):
        def one(step, carry):
            row_copy(src, dst, send, recv, step).wait_recv()
            return carry

        lax.fori_loop(1, nby, one, 0)

    def wait_row_send(src, dst, send, recv):
        def one(step, carry):
            row_copy(src, dst, send, recv, step).wait_send()
            return carry

        lax.fori_loop(1, nby, one, 0)

    start_row(gsend, gpool, g_send, g_recv)

    for k in range(27):
        wback[k // 9, :, 128 * (k % 9) : 128 * (k % 9) + 128] = weight[26 - k]
    for q in range(8):
        wdcat[q // 2, :, 128 * (q % 2) : 128 * (q % 2) + 128] = down[q]
    local_pools()
    for copy in first:
        copy.wait_recv()
    remote_pools(0)
    rims()
    columns(col)

    def forward(b, carry):
        total = None
        for o1 in range(3):
            rows = col[pl.ds(b * 10 + o1, 8)].reshape(512, 1152)
            term = jnp.dot(rows, weight[9 * o1 : 9 * o1 + 9].reshape(1152, 128), preferred_element_type=F32)
            total = term if total is None else total + term
        slope[b] = total.reshape(8, 64, 128)
        return carry

    lax.fori_loop(0, 2, forward, 0)

    def activate(i, carry):
        b, a1 = i // 4, lax.rem(i, 4)
        for p1 in (0, 1):
            x = 2 * a1 + p1
            pre = slope[b, x]
            g = jax.nn.sigmoid(pre)
            act = (pre * g).astype(BF16)
            hid_out[b, x] = act
            lines = act.astype(F32).reshape(4, 2, 8, 128)
            for p2 in (0, 1):
                at_row = pl.multiple_of(b * 128 + a1 * 32, 32)
                hpart[2 * p1 + p2, pl.ds(at_row, 32), :] = lines[:, p2].reshape(32, 128).astype(BF16)
            slope[b, x] = g * (1.0 + pre * (1.0 - g))
        return carry

    lax.fori_loop(0, 8, activate, 0)

    total = None
    for q in range(4):
        term = jnp.dot(hpart[q], wdcat[q], preferred_element_type=F32)
        total = term if total is None else total + term
    wide[0] = total[:, :128]
    wide[1] = total[:, 128:]
    reduced = wide[0, pl.ds(0, 128, stride=2), :] + wide[1, pl.ds(1, 128, stride=2), :]
    reduced = reduced.astype(BF16).reshape(2, 64, 128)

    for step in range(nby):
        to = lax.rem(c + step, nby)
        second = jnp.full((64, 128), cdest[1], jnp.int32) == to
        block = jnp.where(second, reduced[1].astype(F32), reduced[0].astype(F32)).astype(BF16)
        if step == 0:
            rpool[0] = block
        else:
            rsend[step] = block
    start_row(rsend, rpool, c_send, c_recv)

    wait_row_recv(gsend, gpool, g_send, g_recv)
    wide[...] = jnp.zeros((2, 256, 128), F32)
    for b in (0, 1):
        block = gpool[lax.rem(c - cdest[b] + nby, nby)].astype(F32)
        wide[0, pl.ds(128 * b, 64, stride=2), :] = block
        wide[1, pl.ds(128 * b + 1, 64, stride=2), :] = block
    cgx[:, :128] = wide[0].astype(BF16)
    cgx[:, 128:] = wide[1].astype(BF16)
    for q in range(4):
        up[q] = lax.dot_general(cgx[...], wdcat[q], (((1,), (1,)), ((), ())), preferred_element_type=F32)

    def pre_grad(i, carry):
        b, a1 = i // 4, lax.rem(i, 4)
        for p1 in (0, 1):
            x = 2 * a1 + p1
            at_row = pl.multiple_of(b * 128 + a1 * 32, 32)
            parts = [up[2 * p1 + p2, pl.ds(at_row, 32), :].reshape(4, 8, 128) for p2 in (0, 1)]
            back = jnp.stack(parts, axis=1).reshape(64, 128)
            grad = ((gout[b, x].astype(F32) + back) * slope[b, x]).astype(BF16)
            gbf[b, x] = grad
            pad[b, x + 1, 1:9, 1:9, :] = grad.astype(F32).reshape(8, 8, 128)
        return carry

    lax.fori_loop(0, 8, pre_grad, 0)
    stage_faces(1)
    second_halo = halo_copies(1)
    for copy in second_halo:
        copy.start()

    def contracted(left, right):
        return lax.dot_general(left, right, (((0,), (0,)), ((), ())), preferred_element_type=F32)

    for q in range(4):
        both = contracted(hpart[q], cgx[...])
        for l in (0, 1):
            n = 2 * q + l
            arf[n // 3, 1152 + 128 * (n % 3) : 1280 + 128 * (n % 3)] = both[:, 128 * l : 128 * l + 128]
    misfits = jnp.int32(0)
    for b in (0, 1):
        for offset in OFFSETS:
            good = fits_grid(nb[b, offset_index(offset)], offset[0], offset[1])
            misfits = misfits + jnp.where(good, 0, 1)
    arf[2, 1408:1536] = jnp.full((128, 128), misfits, jnp.int32).astype(F32)

    my_half = pl.multiple_of(core * HALF_ROWS, HALF_ROWS)
    your_half = pl.multiple_of((1 - core) * HALF_ROWS, HALF_ROWS)

    def core_copy(part):
        return pltpu.make_async_remote_copy(
            src_ref=s0.at[part], dst_ref=r0.at[part], send_sem=core_send.at[0, part], recv_sem=core_recv.at[0, part],
            device_id=other_core, device_id_type=MESH,
        )

    def core_back(part):
        return pltpu.make_async_remote_copy(
            src_ref=fin.at[core, part], dst_ref=fin.at[core, part], send_sem=core_send.at[1, part],
            recv_sem=core_recv.at[1, part], device_id=other_core, device_id_type=MESH,
        )

    def hop(phase, part, src, dst, axis, step):
        return pltpu.make_async_remote_copy(
            src_ref=src, dst_ref=dst, send_sem=ar_send.at[phase, part, step], recv_sem=ar_recv.at[phase, part, step],
            device_id=moved(axis, step), device_id_type=MESH,
        )

    def hops(phase, part):
        a1, a2, a3 = ROUTES[part]
        out = []
        for step in range(1, size[(a1, a2, a3, a2, a1)[phase]]):
            if phase == 0:
                to = lax.rem(at[a1] + step, size[a1])
                out.append(hop(0, part, s1.at[part, to], r1.at[part, step], a1, step))
            elif phase == 1:
                to = lax.rem(at[a2] + step, size[a2])
                out.append(hop(1, part, s2.at[part, to], r2.at[part, step], a2, step))
            elif phase == 2:
                out.append(hop(2, part, r3.at[part, 0], r3.at[part, step], a3, step))
            elif phase == 3:
                place = fin.at[core, part, at[a1], at[a2]]
                out.append(hop(3, part, place, place, a2, step))
            else:
                place = fin.at[core, part, at[a1]]
                out.append(hop(4, part, place, place, a1, step))
        return out

    def run_hops(phase, part):
        for copy in hops(phase, part):
            copy.start()

    def land_hops(phase, part):
        for copy in hops(phase, part):
            copy.wait_recv()

    n1, n2 = nx, nx
    rows1, rows2 = HALF_ROWS // n1, HALF_ROWS // (n1 * n2)

    for part in range(3):
        def weight_grad(m, carry, part=part):
            lanes = pl.ds(pl.multiple_of(m * 128, 128), 128)
            total = None
            for b in (0, 1):
                rows = col[10 * b + part : 10 * b + part + 8, :, lanes].reshape(512, 128)
                term = contracted(rows, gbf[b].reshape(512, 128))
                total = term if total is None else total + term
            arf[part, pl.ds(pl.multiple_of(m * 128, 128), 128), :] = total
            return carry

        lax.fori_loop(0, 9, weight_grad, 0)
        s0[part] = arf[part, pl.ds(your_half, HALF_ROWS), :].astype(BF16)
        core_copy(part).start()

    for part in range(3):
        core_copy(part).wait_recv()
        hf[part] = arf[part, pl.ds(my_half, HALF_ROWS), :] + r0[part].astype(F32)
        s1[part] = hf[part].astype(BF16).reshape(n1, rows1, 128)
        run_hops(0, part)

    local_pools()
    for copy in second_halo:
        copy.wait_recv()
    remote_pools(1)
    rims()

    for part in range(3):
        land_hops(0, part)
        mine = hf[part, pl.ds(pl.multiple_of(at[ROUTES[part][0]] * rows1, rows1), rows1), :]
        for step in range(1, n1):
            mine = mine + r1[part, step].astype(F32)
        t1f[part] = mine.reshape(n2, rows2, 128)
        s2[part] = mine.astype(BF16).reshape(n2, rows2, 128)
        run_hops(1, part)

    columns(colg)

    for part in range(3):
        land_hops(1, part)
        mine = t1f[part, at[ROUTES[part][1]]]
        for step in range(1, n2):
            mine = mine + r2[part, step].astype(F32)
        r3[part, 0] = mine.astype(BF16)
        run_hops(2, part)

    def backward(b, carry):
        total = None
        for o1 in range(3):
            rows = colg[pl.ds(b * 10 + o1, 8)].reshape(512, 1152)
            term = lax.dot_general(rows, wback[o1], (((1,), (1,)), ((), ())), preferred_element_type=F32)
            total = term if total is None else total + term
        gfeat_out[b] = total.astype(BF16).reshape(8, 64, 128)
        return carry

    backward(0, 0)

    for part in range(3):
        a1, a2, a3 = ROUTES[part]
        land_hops(2, part)
        whole = None
        for place in range(size[a3]):
            term = r3[part, lax.rem(at[a3] - place + size[a3], size[a3])].astype(F32)
            whole = term if whole is None else whole + term
        fin[core, part, at[a1], at[a2]] = (whole * (1.0 / (nbx * nby))).astype(BF16)
        run_hops(3, part)

    backward(1, 0)

    for part in range(3):
        land_hops(3, part)
        run_hops(4, part)

    wait_row_recv(rsend, rpool, c_send, c_recv)
    for m in (0, 1):
        coarse_out[m] = rpool[lax.rem(c - cfrom[m] + nby, nby)]

    for part in range(3):
        land_hops(4, part)
        core_back(part).start()
    for part in range(3):
        core_back(part).wait_recv()
        low = fin[0, part].reshape(HALF_ROWS, 128).astype(F32).reshape(6, 128, 128)
        high = fin[1, part].reshape(HALF_ROWS, 128).astype(F32).reshape(6, 128, 128)
        gw_out[9 * part : 9 * part + 6] = low
        gw_out[9 * part + 6 : 9 * part + 9] = high[:3]
        if part < 2:
            gd_out[3 * part : 3 * part + 3] = high[3:]
        else:
            gd_out[6:8] = high[3:5]
            flag_out[...] = high[5, :8]

    for copy in first + second_halo:
        copy.wait_send()
    wait_row_send(gsend, gpool, g_send, g_recv)
    wait_row_send(rsend, rpool, c_send, c_recv)
    for part in range(3):
        core_copy(part).wait_send()
        core_back(part).wait_send()
        for phase in range(5):
            for copy in hops(phase, part):
                copy.wait_send()


def grid_path(
    sizes, features, weight, down_weight, grad_out, grad_coarse, neighbours, send_list, coarse_dest, coarse_from
):
    nx, ny, nz = sizes
    nby = nx * nz
    rows1, rows2 = HALF_ROWS // nx, HALF_ROWS // (nx * nx)
    vmem, smem = pl.BlockSpec(memory_space=pltpu.VMEM), pl.BlockSpec(memory_space=pltpu.SMEM)
    hidden, coarse, grad_features, grad_weight, grad_down, flag = pl.pallas_call(
        functools.partial(section_kernel, sizes),
        out_shape=[
            jax.ShapeDtypeStruct((2, 8, 64, 128), BF16),
            jax.ShapeDtypeStruct((2, 64, 128), BF16),
            jax.ShapeDtypeStruct((2, 8, 64, 128), BF16),
            jax.ShapeDtypeStruct((27, 128, 128), F32),
            jax.ShapeDtypeStruct((8, 128, 128), F32),
            jax.ShapeDtypeStruct((8, 128), F32),
        ],
        in_specs=[smem] * 4 + [vmem] * 5,
        out_specs=[vmem] * 6,
        scratch_shapes=[
            pltpu.VMEM((3, 10, 10, 16, 128), F32),
            pltpu.VMEM((20, 64, 1152), BF16),
            pltpu.VMEM((20, 64, 1152), BF16),
            pltpu.VMEM((2, 21, 8, 8, 128), F32),
            pltpu.VMEM((2, 21, 8, 8, 128), F32),
            pltpu.VMEM((4, 21, 8, 128), F32),
            pltpu.VMEM((2, 2, 128, 128), BF16),
            pltpu.VMEM((2, 2, 128, 128), BF16),
            pltpu.VMEM((2, 4, 16, 128), BF16),
            pltpu.VMEM((2, 2, 128, 128), BF16),
            pltpu.VMEM((2, 2, 128, 128), BF16),
            pltpu.VMEM((2, 4, 16, 128), BF16),
            pltpu.VMEM((nby, 64, 128), BF16),
            pltpu.VMEM((nby, 64, 128), BF16),
            pltpu.VMEM((nby, 64, 128), BF16),
            pltpu.VMEM((nby, 64, 128), BF16),
            pltpu.VMEM((3, 128, 1152), BF16),
            pltpu.VMEM((4, 128, 256), BF16),
            pltpu.VMEM((2, 8, 64, 128), F32),
            pltpu.VMEM((4, 256, 128), BF16),
            pltpu.VMEM((2, 256, 128), F32),
            pltpu.VMEM((256, 256), BF16),
            pltpu.VMEM((4, 256, 128), F32),
            pltpu.VMEM((2, 8, 64, 128), BF16),
            pltpu.VMEM((3, PART_ROWS, 128), F32),
            pltpu.VMEM((3, HALF_ROWS, 128), BF16),
            pltpu.VMEM((3, HALF_ROWS, 128), BF16),
            pltpu.VMEM((3, HALF_ROWS, 128), F32),
            pltpu.VMEM((3, nx, rows1, 128), BF16),
            pltpu.VMEM((3, nx, rows1, 128), BF16),
            pltpu.VMEM((3, nx, rows2, 128), F32),
            pltpu.VMEM((3, nx, rows2, 128), BF16),
            pltpu.VMEM((3, nx, rows2, 128), BF16),
            pltpu.VMEM((3, nx, rows2, 128), BF16),
            pltpu.VMEM((2, 3, nx, nx, rows2, 128), BF16),
            pltpu.SemaphoreType.DMA((2, 8)),
            pltpu.SemaphoreType.DMA((2, 8)),
            pltpu.SemaphoreType.DMA((nby,)),
            pltpu.SemaphoreType.DMA((nby,)),
            pltpu.SemaphoreType.DMA((nby,)),
            pltpu.SemaphoreType.DMA((nby,)),
            pltpu.SemaphoreType.DMA((5, 3, nx)),
            pltpu.SemaphoreType.DMA((5, 3, nx)),
            pltpu.SemaphoreType.DMA((2, 3)),
            pltpu.SemaphoreType.DMA((2, 3)),
        ],
        compiler_params=pltpu.CompilerParams(
            collective_id=0, has_side_effects=True, vmem_limit_bytes=48 * 2**20
        ),
        cost_estimate=pl.CostEstimate(flops=3 * 10**9, bytes_accessed=6 * 10**6, transcendentals=2**17),
    )(
        neighbours, send_list, coarse_dest, coarse_from,
        features.reshape(2, 8, 64, 128), weight, down_weight, grad_out.reshape(2, 8, 64, 128), grad_coarse,
    )
    return (
        (hidden.reshape(features.shape), coarse, grad_features.reshape(features.shape), grad_weight, grad_down),
        flag[0, 0],
    )


def per_device(sizes, *operands):
    results, misfits = grid_path(sizes, *operands)
    return lax.cond(misfits > 0, lambda: general_path(*operands), lambda: results)


def solution(mesh):
    nby = mesh.shape["by"]
    nx = {16: 4, 4: 2}[nby]
    sizes = (nx, mesh.shape["bx"] // 2, nby // nx)
    in_specs = (
        P(("bx", "by"), None, None, None, None),
        P(),
        P(),
        P(("bx", "by"), None, None, None, None),
        P(("bx", "by"), None, None),
        P(("bx", "by"), None),
        P(("bx", "by"), None),
        P(("bx", "by")),
        P(("bx", "by")),
    )
    out_specs = (
        P(("bx", "by"), None, None, None, None),
        P(("bx", "by"), None, None),
        P(("bx", "by"), None, None, None, None),
        P(),
        P(),
    )
    return jax.shard_map(
        functools.partial(per_device, sizes), mesh=mesh, in_specs=in_specs, out_specs=out_specs, check_vma=False
    )
```

profile of v0, /device:TPU:1, one launch (start us, length us, event | category | flops | bytes accessed | tf_op | source)
XLA Modules:
  0.0 74.2 jit_solution(17452172168361295973)
XLA Ops:
  7.2 0.8 %copy.391.sl = s32[9,2]{1,0:T(8,128)S(1)} copy(s32[9,2]{0,1:T(2,128)} %param.21) | data formatting | bytes 144 | tf_op args[6]
  7.9 0.0 copy-start
  7.9 0.0 copy-start.10
  7.9 0.0 copy-start.39
  7.9 0.0 copy-start.72
  7.9 0.0 copy-start.79
  8.0 0.0 copy-start.80
  8.0 53.9 %shard_map.132 = (bf16[2,8,64,128]{3,2,1,0:T(8,128)(2,1)S(1)}, bf16[2,64,128]{2,1,0:T(8,128)(2,1)S(1)}, bf16[2,8,64,128]{3,2,1,0:T(8,128)(2,1)S(1)}, f32[27,128,...) custom-call(s32[2,27]{1,0:T(2,128)} %nb.1, s32[9,2]{1,0:T(8,128)S(1)} %copy.391.sl, s32[2]{0:T(128)} %cdest.1, ...), custom_call_target="tpu_custom_call" | custom-call | flops 3000000000 | bytes 6000000 | tf_op jit(solution)/shard_map/pallas_call | solution.py:722
  61.9 0.5 slice.711
  63.1 0.0 copy-done
  63.1 0.0 copy-done.10
  63.1 0.0 copy-done.39
  63.1 0.0 copy-done.72
  63.1 0.0 copy-done.79
  63.1 0.0 copy-done.80
  63.1 0.2 conditional.1
  63.4 0.7 copy.608
  64.1 0.6 copy.609
  64.7 0.7 copy.610
  65.4 1.2 %copy.611 = f32[27,128,128]{2,1,0:T(8,128)} copy(f32[27,128,128]{2,1,0:T(8,128)S(1)} %get-tuple-element.365) | data formatting | bytes 3538944
  66.6 0.8 %copy.612 = f32[8,128,128]{2,1,0:T(8,128)} copy(f32[8,128,128]{2,1,0:T(8,128)S(1)} %get-tuple-element.366) | data formatting | bytes 1048576
Async XLA Ops:
  7.9 55.1 %copy-start = (bf16[2,8,8,8,128]{4,3,2,1,0:T(8,128)(2,1)S(1)}, bf16[2,8,8,8,128]{4,3,2,1,0:T(8,128)(2,1)}, u32[]{:S(2)}) copy-start(bf16[2,8,8,8,128]{4,3,2,1,0:T(8,128)(2,1)} %param.15) | copy-start | bytes 786436
  7.9 55.1 %copy-start.10 = (bf16[8,128,128]{2,1,0:T(8,128)(2,1)S(1)}, bf16[8,128,128]{2,1,0:T(8,128)(2,1)}, u32[]{:S(2)}) copy-start(bf16[8,128,128]{2,1,0:T(8,128)(2,1)} %down.1) | copy-start | bytes 786436
  7.9 55.2 %copy-start.39 = (bf16[2,64,128]{2,1,0:T(8,128)(2,1)S(1)}, bf16[2,64,128]{2,1,0:T(8,128)(2,1)}, u32[]{:S(2)}) copy-start(bf16[2,64,128]{2,1,0:T(8,128)(2,1)} %gcoarse.1) | copy-start | bytes 98308
  7.9 55.2 %copy-start.72 = (s32[9,2]{0,1:T(2,128)S(1)}, s32[9,2]{0,1:T(2,128)}, u32[]{:S(2)}) copy-start(s32[9,2]{0,1:T(2,128)} %param.21) | copy-start | bytes 220
  7.9 55.2 %copy-start.79 = (s32[2,27]{1,0:T(2,128)S(1)}, s32[2,27]{1,0:T(2,128)}, u32[]{:S(2)}) copy-start(s32[2,27]{1,0:T(2,128)} %nb.1) | copy-start | bytes 652
  8.0 55.2 %copy-start.80 = (s32[2]{0:T(128)S(1)}, s32[2]{0:T(128)}, u32[]{:S(2)}) copy-start(s32[2]{0:T(128)} %cdest.1) | copy-start | bytes 28
where the time goes:
time: 74.4 us; the launch traced here: 74.2 us
  Pallas kernels  53.9 us (72%)
  between operations  14.7 us (20%)
  local copies, waits for them, and re-layouts  5.33 us (7%)
    pallas_call x1, Pallas kernels, grid_path(): pl.pallas_call(functools.partial(section_kernel, sizes), out_shape=[jax.S...  53.9 us
    unnamed x18, local copies, waits for them, and re-layouts  4.82 us

commit v1 on v0

--- a/solution.py
+++ b/solution.py
@@ -170,10 +170,27 @@
     return build_padded(blocks, face_pool.reshape((-1,) + all_faces.shape[2:]), neighbours)
 
 
-def prior_count(owners, columns):
-    onehot = (owners[:, None] == jnp.arange(columns, dtype=jnp.int32)[None, :]).astype(jnp.int32)
-    before = jnp.cumsum(onehot, axis=0) - onehot
-    return jnp.sum(before * onehot, axis=1)
+def row_gathered(blocks):
+    count = lax.axis_size("by")
+    me = lax.axis_index("by")
+
+    def one(step, state):
+        held, gathered = state
+        held = lax.ppermute(held, "by", [(i, (i + 1) % count) for i in range(count)])
+        return held, gathered.at[lax.rem(me - step + count, count)].set(held)
+
+    gathered = jnp.zeros((count,) + blocks.shape, blocks.dtype).at[me].set(blocks)
+    return lax.fori_loop(1, count, one, (blocks, gathered))[1]
+
+
+def summed(terms):
+    for axis in ("bx", "by"):
+        count, distance = lax.axis_size(axis), 1
+        while distance < count:
+            pairs = [(i, i ^ distance) for i in range(count)]
+            terms = [term + lax.ppermute(term, axis, pairs) for term in terms]
+            distance *= 2
+    return terms
 
 
 def general_path(
@@ -187,24 +204,16 @@
     coarse_dest,
     coarse_from,
 ):
+    send_list = send_list.T
     block_count, edge_len, channels = (features.shape[0], features.shape[1], features.shape[-1])
     device_total = lax.axis_size("bx") * lax.axis_size("by")
     padded_in = padded_for(features, send_list, neighbours)
     preact = conv_rows(padded_in, weight, 1).reshape(features.shape)
     hidden = jax.nn.silu(preact).astype(jnp.bfloat16)
     reduced = down_blocks(hidden, down_weight).astype(jnp.bfloat16)
-    columns = lax.axis_size("by")
-    per_peer = -(-block_count // columns)
-    send_rank = prior_count(coarse_dest, columns)
-    recv_rank = prior_count(coarse_from, columns)
-    outgoing = jnp.zeros((columns * per_peer,) + reduced.shape[1:], jnp.bfloat16)
-    outgoing = outgoing.at[coarse_dest * per_peer + send_rank].set(reduced)
-    arrived = lax.all_to_all(outgoing, "by", split_axis=0, concat_axis=0, tiled=True)
-    coarse = arrived[coarse_from * per_peer + recv_rank]
-    returning = jnp.zeros((columns * per_peer,) + grad_coarse.shape[1:], jnp.bfloat16)
-    returning = returning.at[coarse_from * per_peer + recv_rank].set(grad_coarse)
-    came_back = lax.all_to_all(returning, "by", split_axis=0, concat_axis=0, tiled=True)
-    coarse_grad_here = came_back[coarse_dest * per_peer + send_rank]
+    slots = jnp.arange(block_count)
+    coarse = row_gathered(reduced)[coarse_from, slots]
+    coarse_grad_here = row_gathered(grad_coarse)[coarse_dest, slots]
     flat_grad = coarse_grad_here.reshape(-1, channels)
     down_terms = jnp.stack([contract(rows_in, flat_grad) for rows_in in children(hidden)])
     sigmoid_pre = jax.nn.sigmoid(preact)
@@ -222,7 +231,7 @@
             for offset in OFFSETS
         ]
     )
-    weight_total, down_total = lax.psum((weight_terms, down_terms), ("bx", "by"))
+    weight_total, down_total = summed([weight_terms, down_terms])
     return (hidden, coarse, grad_features, weight_total / device_total, down_total / device_total)
 
 
@@ -247,14 +256,14 @@
 
 def section_kernel(
     sizes,
-    nb, sl, cdest, cfrom,
-    feat, weight, down, gout, gcoarse,
-    hid_out, coarse_out, gfeat_out, gw_out, gd_out, flag_out,
+    nb_in, sl_in, cdest_in, cfrom_in, feat_in, weight_in, down_in, gout_in, gcoarse_in,
+    hid_out, coarse_out, gfeat_out, fin,
+    nb, sl, cdest, cfrom, feat, weight, down, gout, gcoarse, in_sem,
     pad, col, colg, xpool, ypool, cpool,
     xs, ys, cs, xr, yr, cr,
     gsend, gpool, rsend, rpool,
-    wback, wdcat, slope, hpart, wide, cgx, up, gbf,
-    arf, s0, r0, hf, s1, r1, t1f, s2, r2, r3, fin,
+    wback, wdcat, slope, hpart, wide, cgx, up, gcat,
+    arf, s0, r0, hf, s1, r1, t1f, s2, r2, r3,
     halo_send, halo_recv, g_send, g_recv, c_send, c_recv, ar_send, ar_recv, core_send, core_recv,
 ):
     nx, ny, nz = sizes
@@ -274,6 +283,16 @@
         return (lax.rem(r + dr + nbx, nbx), lax.rem(c + dc + nby, nby))
 
     around = [(dr, dc) for dr in (-1, 0, 1) for dc in (-1, 0, 1) if (dr, dc) != (0, 0)]
+
+    staged = {}
+    pairs = (
+        ("sl", sl_in, sl), ("feat", feat_in, feat), ("cfrom", cfrom_in, cfrom), ("gcoarse", gcoarse_in, gcoarse),
+        ("nb", nb_in, nb), ("down", down_in, down), ("weight", weight_in, weight), ("cdest", cdest_in, cdest),
+        ("gout", gout_in, gout),
+    )
+    for n, (name, src, dst) in enumerate(pairs):
+        staged[name] = pltpu.make_async_copy(src, dst, in_sem.at[n])
+        staged[name].start()
 
     barrier = pltpu.get_barrier_semaphore()
 
@@ -296,7 +315,6 @@
         pad[b, x + 1, 1:9, 1:9, :] = feat[b, x].astype(F32).reshape(8, 8, 128)
         return carry
 
-    lax.fori_loop(0, 16, fill_interior, 0)
     pad[2, 1:9, 1:9] = jnp.zeros((8, 8, 16, 128), F32)
     for side in (0, 1):
         xpool[side, NONE] = jnp.zeros((8, 8, 128), F32)
@@ -311,16 +329,16 @@
         for side in (0, 1):
             step = 2 * side - 1
             for j in (0, 1):
-                bx_block = jnp.maximum(sl[(step + 1) * 3 + 1, j], 0)
+                bx_block = jnp.maximum(sl[j, (step + 1) * 3 + 1], 0)
                 face = pad[bx_block, edge[side], 1:9, 1:9, :]
                 xs[t, side, 64 * j : 64 * j + 64] = face.reshape(64, 128).astype(BF16)
-                by_block = jnp.maximum(sl[3 + step + 1, j], 0)
+                by_block = jnp.maximum(sl[j, 3 + step + 1], 0)
                 face = pad[by_block, 1:9, edge[side], 1:9, :]
                 ys[t, side, 64 * j : 64 * j + 64] = face.reshape(64, 128).astype(BF16)
         for sx in (0, 1):
             for sy in (0, 1):
                 row = 2 * sx * 3 + 2 * sy
-                lines = [pad[jnp.maximum(sl[row, j], 0), edge[sx], edge[sy], 1:9, :] for j in (0, 1)]
+                lines = [pad[jnp.maximum(sl[j, row], 0), edge[sx], edge[sy], 1:9, :] for j in (0, 1)]
                 cs[t, 2 * sx + sy] = jnp.concatenate(lines, axis=0).astype(BF16)
 
     def halo_copies(t):
@@ -410,7 +428,16 @@
 
         lax.fori_loop(0, 20, one, 0)
 
+    for b in (0, 1):
+        for o1 in range(3):
+            for x in (8, 9):
+                gcat[10 * b + (x + o1) % 10, :, 128 * o1 : 128 * o1 + 128] = jnp.zeros((64, 128), BF16)
+    staged["feat"].wait()
+    lax.fori_loop(0, 16, fill_interior, 0)
+    staged["sl"].wait()
     stage_faces(0)
+    staged["cfrom"].wait()
+    staged["gcoarse"].wait()
 
     def stage_gcoarse(step, carry):
         to = lax.rem(c + step, nby)
@@ -453,12 +480,14 @@
         lax.fori_loop(1, nby, one, 0)
 
     start_row(gsend, gpool, g_send, g_recv)
-
+    staged["weight"].wait()
     for k in range(27):
         wback[k // 9, :, 128 * (k % 9) : 128 * (k % 9) + 128] = weight[26 - k]
+    staged["down"].wait()
     for q in range(8):
         wdcat[q // 2, :, 128 * (q % 2) : 128 * (q % 2) + 128] = down[q]
     local_pools()
+    staged["nb"].wait()
     for copy in first:
         copy.wait_recv()
     remote_pools(0)
@@ -493,25 +522,8 @@
 
     lax.fori_loop(0, 8, activate, 0)
 
-    total = None
-    for q in range(4):
-        term = jnp.dot(hpart[q], wdcat[q], preferred_element_type=F32)
-        total = term if total is None else total + term
-    wide[0] = total[:, :128]
-    wide[1] = total[:, 128:]
-    reduced = wide[0, pl.ds(0, 128, stride=2), :] + wide[1, pl.ds(1, 128, stride=2), :]
-    reduced = reduced.astype(BF16).reshape(2, 64, 128)
-
-    for step in range(nby):
-        to = lax.rem(c + step, nby)
-        second = jnp.full((64, 128), cdest[1], jnp.int32) == to
-        block = jnp.where(second, reduced[1].astype(F32), reduced[0].astype(F32)).astype(BF16)
-        if step == 0:
-            rpool[0] = block
-        else:
-            rsend[step] = block
-    start_row(rsend, rpool, c_send, c_recv)
-
+    staged["cdest"].wait()
+    staged["gout"].wait()
     wait_row_recv(gsend, gpool, g_send, g_recv)
     wide[...] = jnp.zeros((2, 256, 128), F32)
     for b in (0, 1):
@@ -531,7 +543,8 @@
             parts = [up[2 * p1 + p2, pl.ds(at_row, 32), :].reshape(4, 8, 128) for p2 in (0, 1)]
             back = jnp.stack(parts, axis=1).reshape(64, 128)
             grad = ((gout[b, x].astype(F32) + back) * slope[b, x]).astype(BF16)
-            gbf[b, x] = grad
+            for o1 in range(3):
+                gcat[b * 10 + x + o1, :, 128 * o1 : 128 * o1 + 128] = grad
             pad[b, x + 1, 1:9, 1:9, :] = grad.astype(F32).reshape(8, 8, 128)
         return carry
 
@@ -608,26 +621,48 @@
     n1, n2 = nx, nx
     rows1, rows2 = HALF_ROWS // n1, HALF_ROWS // (n1 * n2)
 
-    for part in range(3):
-        def weight_grad(m, carry, part=part):
-            lanes = pl.ds(pl.multiple_of(m * 128, 128), 128)
-            total = None
-            for b in (0, 1):
-                rows = col[10 * b + part : 10 * b + part + 8, :, lanes].reshape(512, 128)
-                term = contracted(rows, gbf[b].reshape(512, 128))
-                total = term if total is None else total + term
-            arf[part, pl.ds(pl.multiple_of(m * 128, 128), 128), :] = total
-            return carry
-
-        lax.fori_loop(0, 9, weight_grad, 0)
+    def weight_grad(part):
+        for mm in range(3):
+            m = 3 * part + mm
+            rows = col[:, :, 128 * m : 128 * m + 128].reshape(1280, 128)
+            three = contracted(rows, gcat[...].reshape(1280, 384))
+            for o1 in range(3):
+                arf[part, 128 * (3 * o1 + mm) : 128 * (3 * o1 + mm) + 128] = three[:, 128 * o1 : 128 * o1 + 128]
         s0[part] = arf[part, pl.ds(your_half, HALF_ROWS), :].astype(BF16)
         core_copy(part).start()
 
-    for part in range(3):
+    def start_axes(part):
         core_copy(part).wait_recv()
         hf[part] = arf[part, pl.ds(my_half, HALF_ROWS), :] + r0[part].astype(F32)
         s1[part] = hf[part].astype(BF16).reshape(n1, rows1, 128)
         run_hops(0, part)
+
+    weight_grad(0)
+
+    total = None
+    for q in range(4):
+        term = jnp.dot(hpart[q], wdcat[q], preferred_element_type=F32)
+        total = term if total is None else total + term
+    wide[0] = total[:, :128]
+    wide[1] = total[:, 128:]
+    reduced = wide[0, pl.ds(0, 128, stride=2), :] + wide[1, pl.ds(1, 128, stride=2), :]
+    reduced = reduced.astype(BF16).reshape(2, 64, 128)
+
+    for step in range(nby):
+        to = lax.rem(c + step, nby)
+        second = jnp.full((64, 128), cdest[1], jnp.int32) == to
+        block = jnp.where(second, reduced[1].astype(F32), reduced[0].astype(F32)).astype(BF16)
+        if step == 0:
+            rpool[0] = block
+        else:
+            rsend[step] = block
+    start_row(rsend, rpool, c_send, c_recv)
+
+    weight_grad(1)
+    start_axes(0)
+    weight_grad(2)
+    start_axes(1)
+    start_axes(2)
 
     local_pools()
     for copy in second_halo:
@@ -690,15 +725,6 @@
         core_back(part).start()
     for part in range(3):
         core_back(part).wait_recv()
-        low = fin[0, part].reshape(HALF_ROWS, 128).astype(F32).reshape(6, 128, 128)
-        high = fin[1, part].reshape(HALF_ROWS, 128).astype(F32).reshape(6, 128, 128)
-        gw_out[9 * part : 9 * part + 6] = low
-        gw_out[9 * part + 6 : 9 * part + 9] = high[:3]
-        if part < 2:
-            gd_out[3 * part : 3 * part + 3] = high[3:]
-        else:
-            gd_out[6:8] = high[3:5]
-            flag_out[...] = high[5, :8]
 
     for copy in first + second_halo:
         copy.wait_send()
@@ -712,26 +738,61 @@
                 copy.wait_send()
 
 
+def finish_kernel(hid, coarse, gfeat, fin, hid_out, coarse_out, gfeat_out, gw_out, gd_out, misfits, gw, gd, sem):
+    copies = []
+
+    def leave(src, dst):
+        copies.append(pltpu.make_async_copy(src, dst, sem.at[len(copies)]))
+        copies[-1].start()
+
+    leave(hid, hid_out)
+    leave(coarse, coarse_out)
+    leave(gfeat, gfeat_out)
+    for part in range(3):
+        low = fin[0, part].reshape(HALF_ROWS, 128).astype(F32).reshape(6, 128, 128)
+        high = fin[1, part].reshape(HALF_ROWS, 128).astype(F32).reshape(6, 128, 128)
+        for o1, three in enumerate((low[:3], low[3:], high[:3])):
+            at = pl.ds(9 * o1 + 3 * part, 3)
+            gw[at] = three
+            leave(gw.at[at], gw_out.at[at])
+        kept = 3 if part < 2 else 2
+        gd[3 * part : 3 * part + kept] = high[3 : 3 + kept]
+        leave(gd.at[pl.ds(3 * part, kept)], gd_out.at[pl.ds(3 * part, kept)])
+    count = fin[1, 2].reshape(HALF_ROWS, 128)[640:656].astype(F32)
+    misfits[0] = (jnp.max(count) > 0).astype(jnp.int32)
+    for copy in copies:
+        copy.wait()
+
+
 def grid_path(
     sizes, features, weight, down_weight, grad_out, grad_coarse, neighbours, send_list, coarse_dest, coarse_from
 ):
     nx, ny, nz = sizes
     nby = nx * nz
     rows1, rows2 = HALF_ROWS // nx, HALF_ROWS // (nx * nx)
-    vmem, smem = pl.BlockSpec(memory_space=pltpu.VMEM), pl.BlockSpec(memory_space=pltpu.SMEM)
-    hidden, coarse, grad_features, grad_weight, grad_down, flag = pl.pallas_call(
+    vmem = pl.BlockSpec(memory_space=pltpu.VMEM)
+    hbm, smem = pl.BlockSpec(memory_space=pltpu.HBM), pl.BlockSpec(memory_space=pltpu.SMEM)
+    hidden, coarse, grad_features, grads = pl.pallas_call(
         functools.partial(section_kernel, sizes),
         out_shape=[
             jax.ShapeDtypeStruct((2, 8, 64, 128), BF16),
             jax.ShapeDtypeStruct((2, 64, 128), BF16),
             jax.ShapeDtypeStruct((2, 8, 64, 128), BF16),
-            jax.ShapeDtypeStruct((27, 128, 128), F32),
-            jax.ShapeDtypeStruct((8, 128, 128), F32),
-            jax.ShapeDtypeStruct((8, 128), F32),
+            jax.ShapeDtypeStruct((2, 3, nx, nx, rows2, 128), BF16),
         ],
-        in_specs=[smem] * 4 + [vmem] * 5,
-        out_specs=[vmem] * 6,
+        in_specs=[hbm] * 9,
+        out_specs=[vmem] * 4,
         scratch_shapes=[
+            pltpu.SMEM((2, 27), jnp.int32),
+            pltpu.SMEM((2, LISTS), jnp.int32),
+            pltpu.SMEM((2,), jnp.int32),
+            pltpu.SMEM((2,), jnp.int32),
+            pltpu.VMEM((2, 8, 64, 128), BF16),
+            pltpu.VMEM((27, 128, 128), BF16),
+            pltpu.VMEM((8, 128, 128), BF16),
+            pltpu.VMEM((2, 8, 64, 128), BF16),
+            pltpu.VMEM((2, 64, 128), BF16),
+            pltpu.SemaphoreType.DMA((9,)),
             pltpu.VMEM((3, 10, 10, 16, 128), F32),
             pltpu.VMEM((20, 64, 1152), BF16),
             pltpu.VMEM((20, 64, 1152), BF16),
@@ -755,7 +816,7 @@
             pltpu.VMEM((2, 256, 128), F32),
             pltpu.VMEM((256, 256), BF16),
             pltpu.VMEM((4, 256, 128), F32),
-            pltpu.VMEM((2, 8, 64, 128), BF16),
+            pltpu.VMEM((20, 64, 384), BF16),
             pltpu.VMEM((3, PART_ROWS, 128), F32),
             pltpu.VMEM((3, HALF_ROWS, 128), BF16),
             pltpu.VMEM((3, HALF_ROWS, 128), BF16),
@@ -766,7 +827,6 @@
             pltpu.VMEM((3, nx, rows2, 128), BF16),
             pltpu.VMEM((3, nx, rows2, 128), BF16),
             pltpu.VMEM((3, nx, rows2, 128), BF16),
-            pltpu.VMEM((2, 3, nx, nx, rows2, 128), BF16),
             pltpu.SemaphoreType.DMA((2, 8)),
             pltpu.SemaphoreType.DMA((2, 8)),
             pltpu.SemaphoreType.DMA((nby,)),
@@ -786,15 +846,61 @@
         neighbours, send_list, coarse_dest, coarse_from,
         features.reshape(2, 8, 64, 128), weight, down_weight, grad_out.reshape(2, 8, 64, 128), grad_coarse,
     )
+    hidden, coarse, grad_features, grad_weight, grad_down, misfits = pl.pallas_call(
+        finish_kernel,
+        out_shape=[
+            jax.ShapeDtypeStruct((2, 8, 64, 128), BF16),
+            jax.ShapeDtypeStruct((2, 64, 128), BF16),
+            jax.ShapeDtypeStruct((2, 8, 64, 128), BF16),
+            jax.ShapeDtypeStruct((27, 128, 128), F32),
+            jax.ShapeDtypeStruct((8, 128, 128), F32),
+            jax.ShapeDtypeStruct((1,), jnp.int32),
+        ],
+        in_specs=[vmem] * 4,
+        out_specs=[hbm] * 5 + [smem],
+        scratch_shapes=[
+            pltpu.VMEM((27, 128, 128), F32),
+            pltpu.VMEM((8, 128, 128), F32),
+            pltpu.SemaphoreType.DMA((15,)),
+        ],
+        compiler_params=pltpu.CompilerParams(vmem_limit_bytes=16 * 2**20),
+    )(hidden, coarse, grad_features, grads)
     return (
         (hidden.reshape(features.shape), coarse, grad_features.reshape(features.shape), grad_weight, grad_down),
-        flag[0, 0],
-    )
+        misfits[0],
+    )
+
+
+def duplicate_kernel(count, *refs):
+    sources, targets, sem = refs[:count], refs[count : 2 * count], refs[2 * count]
+    for n in range(count):
+        copy = pltpu.make_async_copy(sources[n], targets[n], sem.at[n])
+        copy.start()
+        copy.wait()
+
+
+def duplicates(arrays):
+    count = len(arrays)
+    hbm = pl.BlockSpec(memory_space=pltpu.HBM)
+    return pl.pallas_call(
+        functools.partial(duplicate_kernel, count),
+        out_shape=[jax.ShapeDtypeStruct(array.shape, array.dtype) for array in arrays],
+        in_specs=[hbm] * count,
+        out_specs=[hbm] * count,
+        scratch_shapes=[pltpu.SemaphoreType.DMA((count,))],
+        compiler_params=pltpu.CompilerParams(has_side_effects=True),
+    )(*arrays)
 
 
 def per_device(sizes, *operands):
+    operands = operands[:6] + (operands[6].T,) + operands[7:]
     results, misfits = grid_path(sizes, *operands)
-    return lax.cond(misfits > 0, lambda: general_path(*operands), lambda: results)
+    _, results = lax.while_loop(
+        lambda state: state[0] > 0,
+        lambda state: (jnp.zeros((), jnp.int32), tuple(duplicates(general_path(*duplicates(operands))))),
+        (misfits, results),
+    )
+    return results
 
 
 def solution(mesh):

time: 74.4 us -> 51.1 us (0.69)
  between operations: 14.7 us -> 0.97 us
  local copies, waits for them, and re-layouts: 5.33 us -> 0.06 us
  Pallas kernels: 53.9 us -> 49.2 us
    pallas_call x1, Pallas kernels: 53.9 us -> 47 us  [grid_path(): pl.pallas_call(functools.partial(section_kernel, sizes), out_shape=[jax.S...]
    unnamed x18, local copies, waits for them, and re-layouts: 4.82 us -> 0.06 us
    pallas_call x0 -> x1, Pallas kernels: none -> 2.2 us  [grid_path(): pl.pallas_call(finish_kernel, out_shape=[jax.ShapeDtypeStruct((2, 8, 64,...]
where the time goes in v1:
time: 51.1 us; the launch traced here: 51 us
  Pallas kernels  49.2 us (96%)
  between operations  0.97 us (2%)
  loops' own time  0.78 us (2%)
    pallas_call x1, Pallas kernels, grid_path(): pl.pallas_call(functools.partial(section_kernel, sizes), out_shape=[jax.S...  47 us
    pallas_call x1, Pallas kernels, grid_path(): pl.pallas_call(finish_kernel, out_shape=[jax.ShapeDtypeStruct((2, 8, 64,...  2.2 us

profile of v1, /device:TPU:1, one launch (start us, length us, event | category | flops | bytes accessed | tf_op | source)
XLA Modules:
  0.0 51.0 jit_solution(11999341038053865928)
XLA Ops:
  0.6 0.0 copy-start.36
  0.6 0.0 copy-start.48
  0.7 0.0 copy-start.50
  0.7 0.0 copy-start.52
  0.7 0.0 copy-start.60
  0.7 0.0 copy-start.124
  0.7 0.0 copy-start.126
  0.7 0.0 copy-start.128
  0.7 0.0 copy-start.130
  0.7 47.0 %shard_map.128 = (bf16[2,8,64,128]{3,2,1,0:T(8,128)(2,1)S(1)}, bf16[2,64,128]{2,1,0:T(8,128)(2,1)S(1)}, bf16[2,8,64,128]{3,2,1,0:T(8,128)(2,1)S(1)}, bf16[2,3,4,4,48,128]{5,4,3,2,1,0:T(8,128)(2,1)S(1)}) custom-call(s32[2,27]{1,0:T(2,128)} %nb_in.1, s32[2,9]{1,0:T(2,128)} %bitcast.987, s32[2]{0:T(128)} %cdest_in.1, s32[2]{0:T(128)} %cfrom_in.1, ...), custom_call_target="tpu_custom_call" | custom-call | flops 3000000000 | bytes 6000000 | tf_op jit(solution)/shard_map/pallas_call | solution.py:775
  47.7 2.2 %shard_map.129 = (bf16[2,8,64,128]{3,2,1,0:T(8,128)(2,1)}, bf16[2,64,128]{2,1,0:T(8,128)(2,1)}, bf16[2,8,64,128]{3,2,1,0:T(8,128)(2,1)}, f32[27,128,128]{2,1,0:T...) custom-call(bf16[2,8,64,128]{3,2,1,0:T(8,128)(2,1)S(1)} %get-tuple-element.332.hid, ...), custom_call_target="tpu_custom_call" | custom-call | tf_op jit(solution)/shard_map/pallas_call | solution.py:849
  49.9 0.0 copy-done.36
  50.0 0.0 copy-done.48
  50.0 0.0 copy-done.50
  50.0 0.0 copy-done.52
  50.0 0.0 copy-done.60
  50.0 0.0 copy-done.124
  50.0 0.0 copy-done.126
  50.0 0.0 copy-done.128
  50.0 0.0 copy-done.130
  50.0 0.8 %while.49 = (s32[]{:T(128)}, bf16[2,8,8,8,128]{4,3,2,1,0:T(8,128)(2,1)}, bf16[2,64,128]{2,1,0:T(8,128)(2,1)}, bf16[2,8,8,8,128]{4,3,2,1,0:T(8,128)(2,1)}, f32[27...) while((s32[]{:T(128)}, ...), condition=%region_8.11_spmd, body=%region_0.10_spmd | while | flops 2914811392 | bytes 400067200 | solution.py:898
Async XLA Ops:
  0.6 49.3 %copy-start.36 = (bf16[27,128,128]{2,1,0:T(8,128)(2,1)S(1)}, bf16[27,128,128]{2,1,0:T(8,128)(2,1)}, u32[]{:S(2)}) copy-start(bf16[27,128,128]{2,1,0:T(8,128)(2,1)} %weight_in.1) | copy-start | bytes 2654212
  0.6 49.3 %copy-start.48 = (bf16[2,8,8,8,128]{4,3,2,1,0:T(8,128)(2,1)S(1)}, bf16[2,8,8,8,128]{4,3,2,1,0:T(8,128)(2,1)}, u32[]{:S(2)}) copy-start(bf16[2,8,8,8,128]{4,3,2,1,0:T(8,128)(2,1)} %param.27) | copy-start | bytes 786436
  0.7 49.3 %copy-start.50 = (bf16[8,128,128]{2,1,0:T(8,128)(2,1)S(1)}, bf16[8,128,128]{2,1,0:T(8,128)(2,1)}, u32[]{:S(2)}) copy-start(bf16[8,128,128]{2,1,0:T(8,128)(2,1)} %down_in.1) | copy-start | bytes 786436
  0.7 49.3 %copy-start.52 = (bf16[2,8,8,8,128]{4,3,2,1,0:T(8,128)(2,1)S(1)}, bf16[2,8,8,8,128]{4,3,2,1,0:T(8,128)(2,1)}, u32[]{:S(2)}) copy-start(bf16[2,8,8,8,128]{4,3,2,1,0:T(8,128)(2,1)} %param.30) | copy-start | bytes 786436
  0.7 49.3 %copy-start.60 = (bf16[2,64,128]{2,1,0:T(8,128)(2,1)S(1)}, bf16[2,64,128]{2,1,0:T(8,128)(2,1)}, u32[]{:S(2)}) copy-start(bf16[2,64,128]{2,1,0:T(8,128)(2,1)} %gcoarse_in.1) | copy-start | bytes 98308
  0.7 49.3 %copy-start.124 = (s32[2,27]{1,0:T(2,128)S(1)}, s32[2,27]{1,0:T(2,128)}, u32[]{:S(2)}) copy-start(s32[2,27]{1,0:T(2,128)} %nb_in.1) | copy-start | bytes 652
  0.7 49.3 %copy-start.126 = (s32[9,2]{0,1:T(2,128)S(1)}, s32[9,2]{0,1:T(2,128)}, u32[]{:S(2)}) copy-start(s32[9,2]{0,1:T(2,128)} %param.33) | copy-start | bytes 220
  0.7 49.3 %copy-start.128 = (s32[2]{0:T(128)S(1)}, s32[2]{0:T(128)}, u32[]{:S(2)}) copy-start(s32[2]{0:T(128)} %cdest_in.1) | copy-start | bytes 28
  0.7 49.3 %copy-start.130 = (s32[2]{0:T(128)S(1)}, s32[2]{0:T(128)}, u32[]{:S(2)}) copy-start(s32[2]{0:T(128)} %cfrom_in.1) | copy-start | bytes 28

commit v2 on v1

--- a/solution.py
+++ b/solution.py
@@ -262,12 +262,13 @@
     pad, col, colg, xpool, ypool, cpool,
     xs, ys, cs, xr, yr, cr,
     gsend, gpool, rsend, rpool,
-    wback, wdcat, slope, hpart, wide, cgx, up, gcat,
-    arf, s0, r0, hf, s1, r1, t1f, s2, r2, r3,
-    halo_send, halo_recv, g_send, g_recv, c_send, c_recv, ar_send, ar_recv, core_send, core_recv,
+    wback, wdcat, small, slope, hpart, wide, cgx, up, gcat,
+    arf, s0, r0, hf, s1, r1, r3,
+    halo_send, halo_recv, g_send, g_recv, c_send, c_recv, plane_send, plane_recv, axis_send, axis_recv, core_send, core_recv,
 ):
     nx, ny, nz = sizes
     nby, nbx = nx * nz, 2 * ny
+    ring = nx
     r, c = lax.axis_index("bx"), lax.axis_index("by")
     core, at = lax.rem(r, 2), {"x": lax.rem(c, nx), "y": r // 2, "z": c // nx}
     size = {"x": nx, "y": ny, "z": nz}
@@ -283,6 +284,34 @@
         return (lax.rem(r + dr + nbx, nbx), lax.rem(c + dc + nby, nby))
 
     around = [(dr, dc) for dr in (-1, 0, 1) for dc in (-1, 0, 1) if (dr, dc) != (0, 0)]
+
+    barrier = pltpu.get_barrier_semaphore()
+
+    met = nby - 1
+    for dr, dc in around:
+        if dr != 0:
+            pl.semaphore_signal(barrier, inc=1, device_id=beside(dr, dc), device_id_type=MESH)
+            met += 1
+
+    def greet(step, carry):
+        pl.semaphore_signal(barrier, inc=1, device_id=(r, lax.rem(c + step, nby)), device_id_type=MESH)
+        return carry
+
+    lax.fori_loop(1, nby, greet, 0)
+
+    def greet_planes(n, carry):
+        y = lax.rem(at["y"] + 1 + n // (ring - 1), ring)
+        step = 1 + lax.rem(n, ring - 1)
+        x, z = lax.rem(at["x"] + step, ring), lax.rem(at["z"] + step, ring)
+        for device in ((y * 2 + core, at["z"] * nx + x), (y * 2 + core, z * nx + at["x"])):
+            pl.semaphore_signal(barrier, inc=1, device_id=device, device_id_type=MESH)
+        return carry
+
+    lax.fori_loop(0, (ring - 1) ** 2, greet_planes, 0)
+    met += 2 * (ring - 1) ** 2
+    for step in range(1, ny):
+        pl.semaphore_signal(barrier, inc=1, device_id=moved("y", step), device_id_type=MESH)
+        met += 1
 
     staged = {}
     pairs = (
@@ -293,22 +322,6 @@
     for n, (name, src, dst) in enumerate(pairs):
         staged[name] = pltpu.make_async_copy(src, dst, in_sem.at[n])
         staged[name].start()
-
-    barrier = pltpu.get_barrier_semaphore()
-
-    def greet(step, carry):
-        pl.semaphore_signal(barrier, inc=1, device_id=(r, lax.rem(c + step, nby)), device_id_type=MESH)
-        return carry
-
-    lax.fori_loop(1, nby, greet, 0)
-    met = nby - 1
-    for dr, dc in around:
-        if dr != 0:
-            pl.semaphore_signal(barrier, inc=1, device_id=beside(dr, dc), device_id_type=MESH)
-            met += 1
-    for step in range(1, ny):
-        pl.semaphore_signal(barrier, inc=1, device_id=moved("y", step), device_id_type=MESH)
-        met += 1
 
     def fill_interior(i, carry):
         b, x = i // 8, lax.rem(i, 8)
@@ -452,32 +465,23 @@
     for copy in first:
         copy.start()
 
-    def row_copy(src, dst, send, recv, step):
-        return pltpu.make_async_remote_copy(
-            src_ref=src.at[step], dst_ref=dst.at[step], send_sem=send.at[step], recv_sem=recv.at[step],
-            device_id=(r, lax.rem(c + step, nby)), device_id_type=MESH,
-        )
-
     def start_row(src, dst, send, recv):
         def one(step, carry):
-            row_copy(src, dst, send, recv, step).start()
+            pltpu.make_async_remote_copy(
+                src_ref=src.at[step], dst_ref=dst.at[step], send_sem=send, recv_sem=recv,
+                device_id=(r, lax.rem(c + step, nby)), device_id_type=MESH,
+            ).start()
             return carry
 
         lax.fori_loop(1, nby, one, 0)
 
-    def wait_row_recv(src, dst, send, recv):
-        def one(step, carry):
-            row_copy(src, dst, send, recv, step).wait_recv()
-            return carry
-
-        lax.fori_loop(1, nby, one, 0)
-
-    def wait_row_send(src, dst, send, recv):
-        def one(step, carry):
-            row_copy(src, dst, send, recv, step).wait_send()
-            return carry
-
-        lax.fori_loop(1, nby, one, 0)
+    def all_of(ref, send, recv):
+        return pltpu.make_async_remote_copy(
+            src_ref=ref, dst_ref=ref, send_sem=send, recv_sem=recv, device_id=other_core, device_id_type=MESH
+        )
+
+    def row_waits(buffer, send, recv):
+        return all_of(buffer.at[pl.ds(1, nby - 1)], send, recv)
 
     start_row(gsend, gpool, g_send, g_recv)
     staged["weight"].wait()
@@ -524,7 +528,7 @@
 
     staged["cdest"].wait()
     staged["gout"].wait()
-    wait_row_recv(gsend, gpool, g_send, g_recv)
+    row_waits(gpool, g_send, g_recv).wait_recv()
     wide[...] = jnp.zeros((2, 256, 128), F32)
     for b in (0, 1):
         block = gpool[lax.rem(c - cdest[b] + nby, nby)].astype(F32)
@@ -549,11 +553,6 @@
         return carry
 
     lax.fori_loop(0, 8, pre_grad, 0)
-    stage_faces(1)
-    second_halo = halo_copies(1)
-    for copy in second_halo:
-        copy.start()
-
     def contracted(left, right):
         return lax.dot_general(left, right, (((0,), (0,)), ((), ())), preferred_element_type=F32)
 
@@ -584,42 +583,45 @@
             recv_sem=core_recv.at[1, part], device_id=other_core, device_id_type=MESH,
         )
 
-    def hop(phase, part, src, dst, axis, step):
+    plane, chunk = ring * ring, HALF_ROWS // (ring * ring)
+
+    def spot(part):
+        a1, a2, _ = ROUTES[part]
+        return at[a1] * ring + at[a2]
+
+    def plane_copy(back, part, step):
+        a1, a2, _ = ROUTES[part]
+        to = dict(at)
+        to[a1] = lax.rem(at[a1] + step // ring, ring)
+        to[a2] = lax.rem(at[a2] + lax.rem(step, ring), ring)
+        if back:
+            src = dst = fin.at[core, part, spot(part)]
+        else:
+            src, dst = s1.at[part, to[a1] * ring + to[a2]], r1.at[part, step]
         return pltpu.make_async_remote_copy(
-            src_ref=src, dst_ref=dst, send_sem=ar_send.at[phase, part, step], recv_sem=ar_recv.at[phase, part, step],
-            device_id=moved(axis, step), device_id_type=MESH,
+            src_ref=src, dst_ref=dst, send_sem=plane_send.at[back, part], recv_sem=plane_recv.at[back, part],
+            device_id=(to["y"] * 2 + core, to["z"] * nx + to["x"]), device_id_type=MESH,
         )
 
-    def hops(phase, part):
-        a1, a2, a3 = ROUTES[part]
-        out = []
-        for step in range(1, size[(a1, a2, a3, a2, a1)[phase]]):
-            if phase == 0:
-                to = lax.rem(at[a1] + step, size[a1])
-                out.append(hop(0, part, s1.at[part, to], r1.at[part, step], a1, step))
-            elif phase == 1:
-                to = lax.rem(at[a2] + step, size[a2])
-                out.append(hop(1, part, s2.at[part, to], r2.at[part, step], a2, step))
-            elif phase == 2:
-                out.append(hop(2, part, r3.at[part, 0], r3.at[part, step], a3, step))
-            elif phase == 3:
-                place = fin.at[core, part, at[a1], at[a2]]
-                out.append(hop(3, part, place, place, a2, step))
-            else:
-                place = fin.at[core, part, at[a1]]
-                out.append(hop(4, part, place, place, a1, step))
-        return out
-
-    def run_hops(phase, part):
-        for copy in hops(phase, part):
-            copy.start()
-
-    def land_hops(phase, part):
-        for copy in hops(phase, part):
-            copy.wait_recv()
-
-    n1, n2 = nx, nx
-    rows1, rows2 = HALF_ROWS // n1, HALF_ROWS // (n1 * n2)
+    def start_copies(back, part):
+        def one(step, carry):
+            plane_copy(back, part, step).start()
+            return carry
+
+        lax.fori_loop(1, plane, one, 0)
+
+    def plane_waits(back, part):
+        landed = fin.at[core, part, pl.ds(0, plane - 1)] if back else r1.at[part, pl.ds(1, plane - 1)]
+        return all_of(landed, plane_send.at[back, part], plane_recv.at[back, part])
+
+    def axis_copies(part):
+        return [
+            pltpu.make_async_remote_copy(
+                src_ref=r3.at[part, 0], dst_ref=r3.at[part, step], send_sem=axis_send.at[part, step],
+                recv_sem=axis_recv.at[part, step], device_id=moved(ROUTES[part][2], step), device_id_type=MESH,
+            )
+            for step in range(1, ring)
+        ]
 
     def weight_grad(part):
         for mm in range(3):
@@ -631,14 +633,37 @@
         s0[part] = arf[part, pl.ds(your_half, HALF_ROWS), :].astype(BF16)
         core_copy(part).start()
 
-    def start_axes(part):
+    def start_plane(part):
         core_copy(part).wait_recv()
         hf[part] = arf[part, pl.ds(my_half, HALF_ROWS), :] + r0[part].astype(F32)
-        s1[part] = hf[part].astype(BF16).reshape(n1, rows1, 128)
-        run_hops(0, part)
+        s1[part] = hf[part].astype(BF16).reshape(plane, chunk, 128)
+        start_copies(0, part)
+
+    def start_axis(part):
+        plane_waits(0, part).wait_recv()
+        mine = hf[part, pl.ds(pl.multiple_of(spot(part) * chunk, chunk), chunk), :]
+        for step in range(1, plane):
+            mine = mine + r1[part, step].astype(F32)
+        r3[part, 0] = mine.astype(BF16)
+        for copy in axis_copies(part):
+            copy.start()
+
+    def start_back(part):
+        a3 = ROUTES[part][2]
+        for copy in axis_copies(part):
+            copy.wait_recv()
+        whole = None
+        for place in range(ring):
+            term = r3[part, lax.rem(at[a3] - place + ring, ring)].astype(F32)
+            whole = term if whole is None else whole + term
+        fin[core, part, spot(part)] = (whole * (1.0 / (nbx * nby))).astype(BF16)
+        start_copies(1, part)
 
     weight_grad(0)
-
+    stage_faces(1)
+    second_halo = halo_copies(1)
+    for copy in second_halo:
+        copy.start()
     total = None
     for q in range(4):
         term = jnp.dot(hpart[q], wdcat[q], preferred_element_type=F32)
@@ -646,48 +671,31 @@
     wide[0] = total[:, :128]
     wide[1] = total[:, 128:]
     reduced = wide[0, pl.ds(0, 128, stride=2), :] + wide[1, pl.ds(1, 128, stride=2), :]
-    reduced = reduced.astype(BF16).reshape(2, 64, 128)
-
-    for step in range(nby):
-        to = lax.rem(c + step, nby)
-        second = jnp.full((64, 128), cdest[1], jnp.int32) == to
-        block = jnp.where(second, reduced[1].astype(F32), reduced[0].astype(F32)).astype(BF16)
-        if step == 0:
-            rpool[0] = block
-        else:
-            rsend[step] = block
+    small[...] = reduced.astype(BF16).reshape(2, 64, 128)
+
+    def stage_reduced(step, carry):
+        rsend[step] = small[jnp.where(cdest[1] == lax.rem(c + step, nby), 1, 0)]
+        return carry
+
+    lax.fori_loop(0, nby, stage_reduced, 0)
+    rpool[0] = rsend[0]
     start_row(rsend, rpool, c_send, c_recv)
 
     weight_grad(1)
-    start_axes(0)
+    start_plane(0)
     weight_grad(2)
-    start_axes(1)
-    start_axes(2)
+    start_plane(1)
+    start_plane(2)
 
     local_pools()
     for copy in second_halo:
         copy.wait_recv()
     remote_pools(1)
     rims()
-
-    for part in range(3):
-        land_hops(0, part)
-        mine = hf[part, pl.ds(pl.multiple_of(at[ROUTES[part][0]] * rows1, rows1), rows1), :]
-        for step in range(1, n1):
-            mine = mine + r1[part, step].astype(F32)
-        t1f[part] = mine.reshape(n2, rows2, 128)
-        s2[part] = mine.astype(BF16).reshape(n2, rows2, 128)
-        run_hops(1, part)
-
+    start_axis(0)
+    start_axis(1)
+    start_axis(2)
     columns(colg)
-
-    for part in range(3):
-        land_hops(1, part)
-        mine = t1f[part, at[ROUTES[part][1]]]
-        for step in range(1, n2):
-            mine = mine + r2[part, step].astype(F32)
-        r3[part, 0] = mine.astype(BF16)
-        run_hops(2, part)
 
     def backward(b, carry):
         total = None
@@ -699,43 +707,31 @@
         return carry
 
     backward(0, 0)
-
     for part in range(3):
-        a1, a2, a3 = ROUTES[part]
-        land_hops(2, part)
-        whole = None
-        for place in range(size[a3]):
-            term = r3[part, lax.rem(at[a3] - place + size[a3], size[a3])].astype(F32)
-            whole = term if whole is None else whole + term
-        fin[core, part, at[a1], at[a2]] = (whole * (1.0 / (nbx * nby))).astype(BF16)
-        run_hops(3, part)
-
+        start_back(part)
     backward(1, 0)
 
-    for part in range(3):
-        land_hops(3, part)
-        run_hops(4, part)
-
-    wait_row_recv(rsend, rpool, c_send, c_recv)
+    row_waits(rpool, c_send, c_recv).wait_recv()
     for m in (0, 1):
         coarse_out[m] = rpool[lax.rem(c - cfrom[m] + nby, nby)]
 
     for part in range(3):
-        land_hops(4, part)
+        plane_waits(1, part).wait_recv()
         core_back(part).start()
     for part in range(3):
         core_back(part).wait_recv()
 
     for copy in first + second_halo:
         copy.wait_send()
-    wait_row_send(gsend, gpool, g_send, g_recv)
-    wait_row_send(rsend, rpool, c_send, c_recv)
+    row_waits(gsend, g_send, g_recv).wait_send()
+    row_waits(rsend, c_send, c_recv).wait_send()
     for part in range(3):
         core_copy(part).wait_send()
         core_back(part).wait_send()
-        for phase in range(5):
-            for copy in hops(phase, part):
-                copy.wait_send()
+        plane_waits(0, part).wait_send()
+        plane_waits(1, part).wait_send()
+        for copy in axis_copies(part):
+            copy.wait_send()
 
 
 def finish_kernel(hid, coarse, gfeat, fin, hid_out, coarse_out, gfeat_out, gw_out, gd_out, misfits, gw, gd, sem):
@@ -769,7 +765,7 @@
 ):
     nx, ny, nz = sizes
     nby = nx * nz
-    rows1, rows2 = HALF_ROWS // nx, HALF_ROWS // (nx * nx)
+    plane, chunk = nx * nx, HALF_ROWS // (nx * nx)
     vmem = pl.BlockSpec(memory_space=pltpu.VMEM)
     hbm, smem = pl.BlockSpec(memory_space=pltpu.HBM), pl.BlockSpec(memory_space=pltpu.SMEM)
     hidden, coarse, grad_features, grads = pl.pallas_call(
@@ -778,7 +774,7 @@
             jax.ShapeDtypeStruct((2, 8, 64, 128), BF16),
             jax.ShapeDtypeStruct((2, 64, 128), BF16),
             jax.ShapeDtypeStruct((2, 8, 64, 128), BF16),
-            jax.ShapeDtypeStruct((2, 3, nx, nx, rows2, 128), BF16),
+            jax.ShapeDtypeStruct((2, 3, plane, chunk, 128), BF16),
         ],
         in_specs=[hbm] * 9,
         out_specs=[vmem] * 4,
@@ -811,6 +807,7 @@
             pltpu.VMEM((nby, 64, 128), BF16),
             pltpu.VMEM((3, 128, 1152), BF16),
             pltpu.VMEM((4, 128, 256), BF16),
+            pltpu.VMEM((2, 64, 128), BF16),
             pltpu.VMEM((2, 8, 64, 128), F32),
             pltpu.VMEM((4, 256, 128), BF16),
             pltpu.VMEM((2, 256, 128), F32),
@@ -821,20 +818,19 @@
             pltpu.VMEM((3, HALF_ROWS, 128), BF16),
             pltpu.VMEM((3, HALF_ROWS, 128), BF16),
             pltpu.VMEM((3, HALF_ROWS, 128), F32),
-            pltpu.VMEM((3, nx, rows1, 128), BF16),
-            pltpu.VMEM((3, nx, rows1, 128), BF16),
-            pltpu.VMEM((3, nx, rows2, 128), F32),
-            pltpu.VMEM((3, nx, rows2, 128), BF16),
-            pltpu.VMEM((3, nx, rows2, 128), BF16),
-            pltpu.VMEM((3, nx, rows2, 128), BF16),
+            pltpu.VMEM((3, plane, chunk, 128), BF16),
+            pltpu.VMEM((3, plane, chunk, 128), BF16),
+            pltpu.VMEM((3, nx, chunk, 128), BF16),
             pltpu.SemaphoreType.DMA((2, 8)),
             pltpu.SemaphoreType.DMA((2, 8)),
-            pltpu.SemaphoreType.DMA((nby,)),
-            pltpu.SemaphoreType.DMA((nby,)),
-            pltpu.SemaphoreType.DMA((nby,)),
-            pltpu.SemaphoreType.DMA((nby,)),
-            pltpu.SemaphoreType.DMA((5, 3, nx)),
-            pltpu.SemaphoreType.DMA((5, 3, nx)),
+            pltpu.SemaphoreType.DMA,
+            pltpu.SemaphoreType.DMA,
+            pltpu.SemaphoreType.DMA,
+            pltpu.SemaphoreType.DMA,
+            pltpu.SemaphoreType.DMA((2, 3)),
+            pltpu.SemaphoreType.DMA((2, 3)),
+            pltpu.SemaphoreType.DMA((3, nx)),
+            pltpu.SemaphoreType.DMA((3, nx)),
             pltpu.SemaphoreType.DMA((2, 3)),
             pltpu.SemaphoreType.DMA((2, 3)),
         ],

time: 51.1 us -> 47.5 us (0.930)
  Pallas kernels: 49.2 us -> 45.6 us
    pallas_call x1, Pallas kernels: 47 us -> 43.4 us  [grid_path(): pl.pallas_call(functools.partial(section_kernel, sizes), out_shape=[jax.S...]
where the time goes in v2:
time: 47.5 us; the launch traced here: 47.4 us
  Pallas kernels  45.6 us (96%)
  between operations  0.97 us (2%)
  loops' own time  0.78 us (2%)
    pallas_call x1, Pallas kernels, grid_path(): pl.pallas_call(functools.partial(section_kernel, sizes), out_shape=[jax.S...  43.4 us
    pallas_call x1, Pallas kernels, grid_path(): pl.pallas_call(finish_kernel, out_shape=[jax.ShapeDtypeStruct((2, 8, 64,...  2.2 us

profile of v2, /device:TPU:1, one launch (start us, length us, event | category | flops | bytes accessed | tf_op | source)
XLA Modules:
  0.0 47.4 jit_solution(13678064353114242036)
XLA Ops:
  0.6 0.0 copy-start.36
  0.6 0.0 copy-start.48
  0.7 0.0 copy-start.50
  0.7 0.0 copy-start.52
  0.7 0.0 copy-start.60
  0.7 0.0 copy-start.124
  0.7 0.0 copy-start.126
  0.7 0.0 copy-start.128
  0.7 0.0 copy-start.130
  0.7 43.4 %shard_map.128 = (bf16[2,8,64,128]{3,2,1,0:T(8,128)(2,1)S(1)}, bf16[2,64,128]{2,1,0:T(8,128)(2,1)S(1)}, bf16[2,8,64,128]{3,2,1,0:T(8,128)(2,1)S(1)}, bf16[2,3,16,48,128]{4,3,2,1,0:T(8,128)(2,1)S(1)}) custom-call(s32[2,27]{1,0:T(2,128)} %nb_in.1, s32[2,9]{1,0:T(2,128)} %bitcast.987, s32[2]{0:T(128)} %cdest_in.1, s32[2]{0:T(128)} %cfrom_in.1, ...), custom_call_target="tpu_custom_call" | custom-call | flops 3000000000 | bytes 6000000 | tf_op jit(solution)/shard_map/pallas_call | solution.py:771
  44.1 2.2 %shard_map.129 = (bf16[2,8,64,128]{3,2,1,0:T(8,128)(2,1)}, bf16[2,64,128]{2,1,0:T(8,128)(2,1)}, bf16[2,8,64,128]{3,2,1,0:T(8,128)(2,1)}, f32[27,128,128]{2,1,0:T...) custom-call(bf16[2,8,64,128]{3,2,1,0:T(8,128)(2,1)S(1)} %get-tuple-element.332.hid, ...), custom_call_target="tpu_custom_call" | custom-call | tf_op jit(solution)/shard_map/pallas_call | solution.py:845
  46.3 0.0 copy-done.36
  46.3 0.0 copy-done.48
  46.3 0.0 copy-done.50
  46.3 0.0 copy-done.52
  46.4 0.0 copy-done.60
  46.4 0.0 copy-done.124
  46.4 0.0 copy-done.126
  46.4 0.0 copy-done.128
  46.4 0.0 copy-done.130
  46.4 0.8 %while.49 = (s32[]{:T(128)}, bf16[2,8,8,8,128]{4,3,2,1,0:T(8,128)(2,1)}, bf16[2,64,128]{2,1,0:T(8,128)(2,1)}, bf16[2,8,8,8,128]{4,3,2,1,0:T(8,128)(2,1)}, f32[27...) while((s32[]{:T(128)}, ...), condition=%region_8.11_spmd, body=%region_0.10_spmd | while | flops 2914811392 | bytes 400067200 | solution.py:894
Async XLA Ops:
  0.6 45.7 %copy-start.36 = (bf16[27,128,128]{2,1,0:T(8,128)(2,1)S(1)}, bf16[27,128,128]{2,1,0:T(8,128)(2,1)}, u32[]{:S(2)}) copy-start(bf16[27,128,128]{2,1,0:T(8,128)(2,1)} %weight_in.1) | copy-start | bytes 2654212
  0.6 45.7 %copy-start.48 = (bf16[2,8,8,8,128]{4,3,2,1,0:T(8,128)(2,1)S(1)}, bf16[2,8,8,8,128]{4,3,2,1,0:T(8,128)(2,1)}, u32[]{:S(2)}) copy-start(bf16[2,8,8,8,128]{4,3,2,1,0:T(8,128)(2,1)} %param.27) | copy-start | bytes 786436
  0.7 45.7 %copy-start.50 = (bf16[8,128,128]{2,1,0:T(8,128)(2,1)S(1)}, bf16[8,128,128]{2,1,0:T(8,128)(2,1)}, u32[]{:S(2)}) copy-start(bf16[8,128,128]{2,1,0:T(8,128)(2,1)} %down_in.1) | copy-start | bytes 786436
  0.7 45.7 %copy-start.52 = (bf16[2,8,8,8,128]{4,3,2,1,0:T(8,128)(2,1)S(1)}, bf16[2,8,8,8,128]{4,3,2,1,0:T(8,128)(2,1)}, u32[]{:S(2)}) copy-start(bf16[2,8,8,8,128]{4,3,2,1,0:T(8,128)(2,1)} %param.30) | copy-start | bytes 786436
  0.7 45.7 %copy-start.60 = (bf16[2,64,128]{2,1,0:T(8,128)(2,1)S(1)}, bf16[2,64,128]{2,1,0:T(8,128)(2,1)}, u32[]{:S(2)}) copy-start(bf16[2,64,128]{2,1,0:T(8,128)(2,1)} %gcoarse_in.1) | copy-start | bytes 98308
  0.7 45.7 %copy-start.124 = (s32[2,27]{1,0:T(2,128)S(1)}, s32[2,27]{1,0:T(2,128)}, u32[]{:S(2)}) copy-start(s32[2,27]{1,0:T(2,128)} %nb_in.1) | copy-start | bytes 652
  0.7 45.7 %copy-start.126 = (s32[9,2]{0,1:T(2,128)S(1)}, s32[9,2]{0,1:T(2,128)}, u32[]{:S(2)}) copy-start(s32[9,2]{0,1:T(2,128)} %param.33) | copy-start | bytes 220
  0.7 45.7 %copy-start.128 = (s32[2]{0:T(128)S(1)}, s32[2]{0:T(128)}, u32[]{:S(2)}) copy-start(s32[2]{0:T(128)} %cdest_in.1) | copy-start | bytes 28
  0.7 45.7 %copy-start.130 = (s32[2]{0:T(128)S(1)}, s32[2]{0:T(128)}, u32[]{:S(2)}) copy-start(s32[2]{0:T(128)} %cfrom_in.1) | copy-start | bytes 28

commit v3 on v2

--- a/solution.py
+++ b/solution.py
@@ -244,6 +244,11 @@
 HALF_ROWS = 768
 
 
+def farthest_first(ring):
+    steps = [(i, j) for i in range(ring) for j in range(ring) if (i, j) != (0, 0)]
+    return sorted(steps, key=lambda step: -sum(min(i, ring - i) for i in step))
+
+
 def fits_grid(p, o1, o2):
     half = p // 2
     good = (half == 0) | (half == NONE // 2)
@@ -262,20 +267,22 @@
     pad, col, colg, xpool, ypool, cpool,
     xs, ys, cs, xr, yr, cr,
     gsend, gpool, rsend, rpool,
-    wback, wdcat, small, slope, hpart, wide, cgx, up, gcat,
+    wback, wpair, wdcat, small, slope, hpart, wide, cgx, up, gcat,
     arf, s0, r0, hf, s1, r1, r3,
     halo_send, halo_recv, g_send, g_recv, c_send, c_recv, plane_send, plane_recv, axis_send, axis_recv, core_send, core_recv,
 ):
     nx, ny, nz = sizes
     nby, nbx = nx * nz, 2 * ny
     ring = nx
+    others = farthest_first(ring)
     r, c = lax.axis_index("bx"), lax.axis_index("by")
     core, at = lax.rem(r, 2), {"x": lax.rem(c, nx), "y": r // 2, "z": c // nx}
     size = {"x": nx, "y": ny, "z": nz}
 
-    def moved(axis, step):
+    def stepped(*steps):
         to = dict(at)
-        to[axis] = lax.rem(at[axis] + step, size[axis])
+        for axis, step in steps:
+            to[axis] = lax.rem(at[axis] + step, ring)
         return (to["y"] * 2 + core, to["z"] * nx + to["x"])
 
     other_core = (r + 1 - 2 * core, c)
@@ -287,31 +294,16 @@
 
     barrier = pltpu.get_barrier_semaphore()
 
-    met = nby - 1
-    for dr, dc in around:
-        if dr != 0:
-            pl.semaphore_signal(barrier, inc=1, device_id=beside(dr, dc), device_id_type=MESH)
-            met += 1
-
-    def greet(step, carry):
-        pl.semaphore_signal(barrier, inc=1, device_id=(r, lax.rem(c + step, nby)), device_id_type=MESH)
-        return carry
-
-    lax.fori_loop(1, nby, greet, 0)
-
-    def greet_planes(n, carry):
-        y = lax.rem(at["y"] + 1 + n // (ring - 1), ring)
-        step = 1 + lax.rem(n, ring - 1)
-        x, z = lax.rem(at["x"] + step, ring), lax.rem(at["z"] + step, ring)
-        for device in ((y * 2 + core, at["z"] * nx + x), (y * 2 + core, z * nx + at["x"])):
-            pl.semaphore_signal(barrier, inc=1, device_id=device, device_id_type=MESH)
-        return carry
-
-    lax.fori_loop(0, (ring - 1) ** 2, greet_planes, 0)
-    met += 2 * (ring - 1) ** 2
-    for step in range(1, ny):
-        pl.semaphore_signal(barrier, inc=1, device_id=moved("y", step), device_id_type=MESH)
-        met += 1
+    greeted = []
+    for i, j in others:
+        greeted.append(stepped(("z", i), ("x", j)))
+        if i != 0:
+            greeted.append(stepped(("y", i), ("z", j)))
+        if i != 0 and j != 0:
+            greeted.append(stepped(("x", i), ("y", j)))
+    greeted += [beside(dr, dc) for dr, dc in around if dr != 0]
+    for device in greeted:
+        pl.semaphore_signal(barrier, inc=1, device_id=device, device_id_type=MESH)
 
     staged = {}
     pairs = (
@@ -356,13 +348,13 @@
 
     def halo_copies(t):
         out = []
-        for side in (0, 1):
-            out.append((xs.at[t, side], xr.at[t, 1 - side], beside(2 * side - 1, 0)))
-        for side in (0, 1):
-            out.append((ys.at[t, side], yr.at[t, 1 - side], beside(0, 2 * side - 1)))
         for sx in (0, 1):
             for sy in (0, 1):
                 out.append((cs.at[t, 2 * sx + sy], cr.at[t, 3 - 2 * sx - sy], beside(2 * sx - 1, 2 * sy - 1)))
+        for side in (0, 1):
+            out.append((ys.at[t, side], yr.at[t, 1 - side], beside(0, 2 * side - 1)))
+        for side in (0, 1):
+            out.append((xs.at[t, side], xr.at[t, 1 - side], beside(2 * side - 1, 0)))
         return [
             pltpu.make_async_remote_copy(
                 src_ref=src, dst_ref=dst, send_sem=halo_send.at[t, n], recv_sem=halo_recv.at[t, n],
@@ -452,28 +444,31 @@
     staged["cfrom"].wait()
     staged["gcoarse"].wait()
 
+    def row_place(step):
+        return lax.rem(at["z"] + step // nx, nz) * nx + lax.rem(at["x"] + lax.rem(step, nx), nx)
+
     def stage_gcoarse(step, carry):
-        to = lax.rem(c + step, nby)
+        to = row_place(step)
         gsend[step] = gcoarse[jnp.where(cfrom[1] == to, 1, 0)]
         return carry
 
     lax.fori_loop(0, nby, stage_gcoarse, 0)
     gpool[0] = gsend[0]
 
-    pl.semaphore_wait(barrier, met)
+    pl.semaphore_wait(barrier, len(greeted))
     first = halo_copies(0)
     for copy in first:
         copy.start()
 
     def start_row(src, dst, send, recv):
-        def one(step, carry):
+        for i, j in others:
             pltpu.make_async_remote_copy(
-                src_ref=src.at[step], dst_ref=dst.at[step], send_sem=send, recv_sem=recv,
-                device_id=(r, lax.rem(c + step, nby)), device_id_type=MESH,
+                src_ref=src.at[i * ring + j], dst_ref=dst.at[i * ring + j], send_sem=send, recv_sem=recv,
+                device_id=stepped(("z", i), ("x", j)), device_id_type=MESH,
             ).start()
-            return carry
-
-        lax.fori_loop(1, nby, one, 0)
+
+    def from_row(by):
+        return lax.rem(at["z"] - by // nx + nz, nz) * nx + lax.rem(at["x"] - lax.rem(by, nx) + nx, nx)
 
     def all_of(ref, send, recv):
         return pltpu.make_async_remote_copy(
@@ -487,11 +482,20 @@
     staged["weight"].wait()
     for k in range(27):
         wback[k // 9, :, 128 * (k % 9) : 128 * (k % 9) + 128] = weight[26 - k]
+    for m in range(9):
+        for o1 in (0, 1):
+            wpair[m, :, 128 * o1 : 128 * o1 + 128] = weight[9 * o1 + m]
     staged["down"].wait()
     for q in range(8):
         wdcat[q // 2, :, 128 * (q % 2) : 128 * (q % 2) + 128] = down[q]
     local_pools()
     staged["nb"].wait()
+    misfits = jnp.int32(0)
+    for b in (0, 1):
+        for offset in OFFSETS:
+            good = fits_grid(nb[b, offset_index(offset)], offset[0], offset[1])
+            misfits = misfits + jnp.where(good, 0, 1)
+    arf[2, 1408:1536] = jnp.full((128, 128), misfits, jnp.int32).astype(F32)
     for copy in first:
         copy.wait_recv()
     remote_pools(0)
@@ -499,12 +503,11 @@
     columns(col)
 
     def forward(b, carry):
-        total = None
-        for o1 in range(3):
-            rows = col[pl.ds(b * 10 + o1, 8)].reshape(512, 1152)
-            term = jnp.dot(rows, weight[9 * o1 : 9 * o1 + 9].reshape(1152, 128), preferred_element_type=F32)
-            total = term if total is None else total + term
-        slope[b] = total.reshape(8, 64, 128)
+        rows = col[pl.ds(b * 10, 9)].reshape(576, 1152)
+        pair = jnp.dot(rows, wpair[...].reshape(1152, 256), preferred_element_type=F32)
+        rows = col[pl.ds(b * 10 + 2, 8)].reshape(512, 1152)
+        last = jnp.dot(rows, weight[18:27].reshape(1152, 128), preferred_element_type=F32)
+        slope[b] = (pair[:512, :128] + pair[64:, 128:] + last).reshape(8, 64, 128)
         return carry
 
     lax.fori_loop(0, 2, forward, 0)
@@ -531,7 +534,7 @@
     row_waits(gpool, g_send, g_recv).wait_recv()
     wide[...] = jnp.zeros((2, 256, 128), F32)
     for b in (0, 1):
-        block = gpool[lax.rem(c - cdest[b] + nby, nby)].astype(F32)
+        block = gpool[from_row(cdest[b])].astype(F32)
         wide[0, pl.ds(128 * b, 64, stride=2), :] = block
         wide[1, pl.ds(128 * b + 1, 64, stride=2), :] = block
     cgx[:, :128] = wide[0].astype(BF16)
@@ -556,17 +559,11 @@
     def contracted(left, right):
         return lax.dot_general(left, right, (((0,), (0,)), ((), ())), preferred_element_type=F32)
 
-    for q in range(4):
+    def down_grad(q):
         both = contracted(hpart[q], cgx[...])
         for l in (0, 1):
             n = 2 * q + l
             arf[n // 3, 1152 + 128 * (n % 3) : 1280 + 128 * (n % 3)] = both[:, 128 * l : 128 * l + 128]
-    misfits = jnp.int32(0)
-    for b in (0, 1):
-        for offset in OFFSETS:
-            good = fits_grid(nb[b, offset_index(offset)], offset[0], offset[1])
-            misfits = misfits + jnp.where(good, 0, 1)
-    arf[2, 1408:1536] = jnp.full((128, 128), misfits, jnp.int32).astype(F32)
 
     my_half = pl.multiple_of(core * HALF_ROWS, HALF_ROWS)
     your_half = pl.multiple_of((1 - core) * HALF_ROWS, HALF_ROWS)
@@ -589,26 +586,18 @@
         a1, a2, _ = ROUTES[part]
         return at[a1] * ring + at[a2]
 
-    def plane_copy(back, part, step):
+    def start_copies(back, part):
         a1, a2, _ = ROUTES[part]
-        to = dict(at)
-        to[a1] = lax.rem(at[a1] + step // ring, ring)
-        to[a2] = lax.rem(at[a2] + lax.rem(step, ring), ring)
-        if back:
-            src = dst = fin.at[core, part, spot(part)]
-        else:
-            src, dst = s1.at[part, to[a1] * ring + to[a2]], r1.at[part, step]
-        return pltpu.make_async_remote_copy(
-            src_ref=src, dst_ref=dst, send_sem=plane_send.at[back, part], recv_sem=plane_recv.at[back, part],
-            device_id=(to["y"] * 2 + core, to["z"] * nx + to["x"]), device_id_type=MESH,
-        )
-
-    def start_copies(back, part):
-        def one(step, carry):
-            plane_copy(back, part, step).start()
-            return carry
-
-        lax.fori_loop(1, plane, one, 0)
+        for i, j in others:
+            if back:
+                src = dst = fin.at[core, part, spot(part)]
+            else:
+                place = lax.rem(at[a1] + i, ring) * ring + lax.rem(at[a2] + j, ring)
+                src, dst = s1.at[part, place], r1.at[part, i * ring + j]
+            pltpu.make_async_remote_copy(
+                src_ref=src, dst_ref=dst, send_sem=plane_send.at[back, part], recv_sem=plane_recv.at[back, part],
+                device_id=stepped((a1, i), (a2, j)), device_id_type=MESH,
+            ).start()
 
     def plane_waits(back, part):
         landed = fin.at[core, part, pl.ds(0, plane - 1)] if back else r1.at[part, pl.ds(1, plane - 1)]
@@ -618,7 +607,7 @@
         return [
             pltpu.make_async_remote_copy(
                 src_ref=r3.at[part, 0], dst_ref=r3.at[part, step], send_sem=axis_send.at[part, step],
-                recv_sem=axis_recv.at[part, step], device_id=moved(ROUTES[part][2], step), device_id_type=MESH,
+                recv_sem=axis_recv.at[part, step], device_id=stepped((ROUTES[part][2], step)), device_id_type=MESH,
             )
             for step in range(1, ring)
         ]
@@ -659,11 +648,18 @@
         fin[core, part, spot(part)] = (whole * (1.0 / (nbx * nby))).astype(BF16)
         start_copies(1, part)
 
-    weight_grad(0)
+    for part in range(3):
+        for q in ((0, 1), (2,), (3,))[part]:
+            down_grad(q)
+        weight_grad(part)
+    for part in range(3):
+        start_plane(part)
     stage_faces(1)
     second_halo = halo_copies(1)
     for copy in second_halo:
         copy.start()
+    local_pools()
+
     total = None
     for q in range(4):
         term = jnp.dot(hpart[q], wdcat[q], preferred_element_type=F32)
@@ -674,27 +670,22 @@
     small[...] = reduced.astype(BF16).reshape(2, 64, 128)
 
     def stage_reduced(step, carry):
-        rsend[step] = small[jnp.where(cdest[1] == lax.rem(c + step, nby), 1, 0)]
+        rsend[step] = small[jnp.where(cdest[1] == row_place(step), 1, 0)]
         return carry
 
     lax.fori_loop(0, nby, stage_reduced, 0)
     rpool[0] = rsend[0]
+
+    for part in range(3):
+        start_axis(part)
     start_row(rsend, rpool, c_send, c_recv)
-
-    weight_grad(1)
-    start_plane(0)
-    weight_grad(2)
-    start_plane(1)
-    start_plane(2)
-
-    local_pools()
+    for copy in first:
+        copy.wait_send()
+    row_waits(gsend, g_send, g_recv).wait_send()
     for copy in second_halo:
         copy.wait_recv()
     remote_pools(1)
     rims()
-    start_axis(0)
-    start_axis(1)
-    start_axis(2)
     columns(colg)
 
     def backward(b, carry):
@@ -710,28 +701,29 @@
     for part in range(3):
         start_back(part)
     backward(1, 0)
+    for copy in second_halo:
+        copy.wait_send()
+    for part in range(3):
+        core_copy(part).wait_send()
+        plane_waits(0, part).wait_send()
+        for copy in axis_copies(part):
+            copy.wait_send()
 
     row_waits(rpool, c_send, c_recv).wait_recv()
     for m in (0, 1):
-        coarse_out[m] = rpool[lax.rem(c - cfrom[m] + nby, nby)]
+        coarse_out[m] = rpool[from_row(cfrom[m])]
 
     for part in range(3):
         plane_waits(1, part).wait_recv()
         core_back(part).start()
     for part in range(3):
+        plane_waits(1, part).wait_send()
+    for part in range(3):
         core_back(part).wait_recv()
 
-    for copy in first + second_halo:
-        copy.wait_send()
-    row_waits(gsend, g_send, g_recv).wait_send()
     row_waits(rsend, c_send, c_recv).wait_send()
     for part in range(3):
-        core_copy(part).wait_send()
         core_back(part).wait_send()
-        plane_waits(0, part).wait_send()
-        plane_waits(1, part).wait_send()
-        for copy in axis_copies(part):
-            copy.wait_send()
 
 
 def finish_kernel(hid, coarse, gfeat, fin, hid_out, coarse_out, gfeat_out, gw_out, gd_out, misfits, gw, gd, sem):
@@ -806,6 +798,7 @@
             pltpu.VMEM((nby, 64, 128), BF16),
             pltpu.VMEM((nby, 64, 128), BF16),
             pltpu.VMEM((3, 128, 1152), BF16),
+            pltpu.VMEM((9, 128, 256), BF16),
             pltpu.VMEM((4, 128, 256), BF16),
             pltpu.VMEM((2, 64, 128), BF16),
             pltpu.VMEM((2, 8, 64, 128), F32),

time: 47.5 us -> 44.8 us (0.943)
  Pallas kernels: 45.6 us -> 42.8 us
    pallas_call x1, Pallas kernels: 43.4 us -> 40.6 us  [grid_path(): pl.pallas_call(functools.partial(section_kernel, sizes), out_shape=[jax.S...]
where the time goes in v3:
time: 44.8 us; the launch traced here: 44.6 us
  Pallas kernels  42.8 us (96%)
  between operations  0.97 us (2%)
  loops' own time  0.78 us (2%)
    pallas_call x1, Pallas kernels, grid_path(): pl.pallas_call(functools.partial(section_kernel, sizes), out_shape=[jax.S...  40.6 us
    pallas_call x1, Pallas kernels, grid_path(): pl.pallas_call(finish_kernel, out_shape=[jax.ShapeDtypeStruct((2, 8, 64,...  2.2 us

profile of v3, /device:TPU:1, one launch (start us, length us, event | category | flops | bytes accessed | tf_op | source)
XLA Modules:
  0.0 44.6 jit_solution(17574589817515123495)
XLA Ops:
  0.6 0.0 copy-start.36
  0.6 0.0 copy-start.48
  0.7 0.0 copy-start.50
  0.7 0.0 copy-start.52
  0.7 0.0 copy-start.60
  0.7 0.0 copy-start.124
  0.7 0.0 copy-start.126
  0.7 0.0 copy-start.128
  0.7 0.0 copy-start.130
  0.7 40.6 %shard_map.128 = (bf16[2,8,64,128]{3,2,1,0:T(8,128)(2,1)S(1)}, bf16[2,64,128]{2,1,0:T(8,128)(2,1)S(1)}, bf16[2,8,64,128]{3,2,1,0:T(8,128)(2,1)S(1)}, bf16[2,3,16,48,128]{4,3,2,1,0:T(8,128)(2,1)S(1)}) custom-call(s32[2,27]{1,0:T(2,128)} %nb_in.1, s32[2,9]{1,0:T(2,128)} %bitcast.987, s32[2]{0:T(128)} %cdest_in.1, s32[2]{0:T(128)} %cfrom_in.1, ...), custom_call_target="tpu_custom_call" | custom-call | flops 3000000000 | bytes 6000000 | tf_op jit(solution)/shard_map/pallas_call | solution.py:763
  41.4 2.2 %shard_map.129 = (bf16[2,8,64,128]{3,2,1,0:T(8,128)(2,1)}, bf16[2,64,128]{2,1,0:T(8,128)(2,1)}, bf16[2,8,64,128]{3,2,1,0:T(8,128)(2,1)}, f32[27,128,128]{2,1,0:T...) custom-call(bf16[2,8,64,128]{3,2,1,0:T(8,128)(2,1)S(1)} %get-tuple-element.332.hid, ...), custom_call_target="tpu_custom_call" | custom-call | tf_op jit(solution)/shard_map/pallas_call | solution.py:838
  43.6 0.0 copy-done.36
  43.6 0.0 copy-done.48
  43.6 0.0 copy-done.50
  43.6 0.0 copy-done.52
  43.6 0.0 copy-done.60
  43.6 0.0 copy-done.124
  43.6 0.0 copy-done.126
  43.7 0.0 copy-done.128
  43.7 0.0 copy-done.130
  43.7 0.8 %while.49 = (s32[]{:T(128)}, bf16[2,8,8,8,128]{4,3,2,1,0:T(8,128)(2,1)}, bf16[2,64,128]{2,1,0:T(8,128)(2,1)}, bf16[2,8,8,8,128]{4,3,2,1,0:T(8,128)(2,1)}, f32[27...) while((s32[]{:T(128)}, ...), condition=%region_8.11_spmd, body=%region_0.10_spmd | while | flops 2914811392 | bytes 400067200 | solution.py:887
Async XLA Ops:
  0.6 43.0 %copy-start.36 = (bf16[27,128,128]{2,1,0:T(8,128)(2,1)S(1)}, bf16[27,128,128]{2,1,0:T(8,128)(2,1)}, u32[]{:S(2)}) copy-start(bf16[27,128,128]{2,1,0:T(8,128)(2,1)} %weight_in.1) | copy-start | bytes 2654212
  0.6 43.0 %copy-start.48 = (bf16[2,8,8,8,128]{4,3,2,1,0:T(8,128)(2,1)S(1)}, bf16[2,8,8,8,128]{4,3,2,1,0:T(8,128)(2,1)}, u32[]{:S(2)}) copy-start(bf16[2,8,8,8,128]{4,3,2,1,0:T(8,128)(2,1)} %param.27) | copy-start | bytes 786436
  0.7 42.9 %copy-start.50 = (bf16[8,128,128]{2,1,0:T(8,128)(2,1)S(1)}, bf16[8,128,128]{2,1,0:T(8,128)(2,1)}, u32[]{:S(2)}) copy-start(bf16[8,128,128]{2,1,0:T(8,128)(2,1)} %down_in.1) | copy-start | bytes 786436
  0.7 42.9 %copy-start.52 = (bf16[2,8,8,8,128]{4,3,2,1,0:T(8,128)(2,1)S(1)}, bf16[2,8,8,8,128]{4,3,2,1,0:T(8,128)(2,1)}, u32[]{:S(2)}) copy-start(bf16[2,8,8,8,128]{4,3,2,1,0:T(8,128)(2,1)} %param.30) | copy-start | bytes 786436
  0.7 42.9 %copy-start.60 = (bf16[2,64,128]{2,1,0:T(8,128)(2,1)S(1)}, bf16[2,64,128]{2,1,0:T(8,128)(2,1)}, u32[]{:S(2)}) copy-start(bf16[2,64,128]{2,1,0:T(8,128)(2,1)} %gcoarse_in.1) | copy-start | bytes 98308
  0.7 42.9 %copy-start.124 = (s32[2,27]{1,0:T(2,128)S(1)}, s32[2,27]{1,0:T(2,128)}, u32[]{:S(2)}) copy-start(s32[2,27]{1,0:T(2,128)} %nb_in.1) | copy-start | bytes 652
  0.7 42.9 %copy-start.126 = (s32[9,2]{0,1:T(2,128)S(1)}, s32[9,2]{0,1:T(2,128)}, u32[]{:S(2)}) copy-start(s32[9,2]{0,1:T(2,128)} %param.33) | copy-start | bytes 220
  0.7 42.9 %copy-start.128 = (s32[2]{0:T(128)S(1)}, s32[2]{0:T(128)}, u32[]{:S(2)}) copy-start(s32[2]{0:T(128)} %cdest_in.1) | copy-start | bytes 28
  0.7 42.9 %copy-start.130 = (s32[2]{0:T(128)S(1)}, s32[2]{0:T(128)}, u32[]{:S(2)}) copy-start(s32[2]{0:T(128)} %cfrom_in.1) | copy-start | bytes 28

commit v4 on v3

--- a/solution.py
+++ b/solution.py
@@ -240,8 +240,8 @@
 NONE = 20
 LISTS = 9
 ROUTES = (("x", "y", "z"), ("y", "z", "x"), ("z", "x", "y"))
-PART_ROWS = 1536
 HALF_ROWS = 768
+GROUPS = (((0, 1), (2, 3), (4, 9)), ((5, 6), (7, 8), (10, 11)))
 
 
 def farthest_first(ring):
@@ -268,8 +268,8 @@
     xs, ys, cs, xr, yr, cr,
     gsend, gpool, rsend, rpool,
     wback, wpair, wdcat, small, slope, hpart, wide, cgx, up, gcat,
-    arf, s0, r0, hf, s1, r1, r3,
-    halo_send, halo_recv, g_send, g_recv, c_send, c_recv, plane_send, plane_recv, axis_send, axis_recv, core_send, core_recv,
+    s0, r0, hf, s1, r1, r3,
+    halo_send, halo_recv, g_send, g_recv, c_send, c_recv, plane_send, plane_recv, back_recv, axis_send, axis_recv, core_send, core_recv,
 ):
     nx, ny, nz = sizes
     nby, nbx = nx * nz, 2 * ny
@@ -301,7 +301,7 @@
             greeted.append(stepped(("y", i), ("z", j)))
         if i != 0 and j != 0:
             greeted.append(stepped(("x", i), ("y", j)))
-    greeted += [beside(dr, dc) for dr, dc in around if dr != 0]
+    greeted = [beside(dr, dc) for dr, dc in around if dr != 0] + greeted
     for device in greeted:
         pl.semaphore_signal(barrier, inc=1, device_id=device, device_id_type=MESH)
 
@@ -495,7 +495,6 @@
         for offset in OFFSETS:
             good = fits_grid(nb[b, offset_index(offset)], offset[0], offset[1])
             misfits = misfits + jnp.where(good, 0, 1)
-    arf[2, 1408:1536] = jnp.full((128, 128), misfits, jnp.int32).astype(F32)
     for copy in first:
         copy.wait_recv()
     remote_pools(0)
@@ -559,26 +558,21 @@
     def contracted(left, right):
         return lax.dot_general(left, right, (((0,), (0,)), ((), ())), preferred_element_type=F32)
 
-    def down_grad(q):
-        both = contracted(hpart[q], cgx[...])
-        for l in (0, 1):
-            n = 2 * q + l
-            arf[n // 3, 1152 + 128 * (n % 3) : 1280 + 128 * (n % 3)] = both[:, 128 * l : 128 * l + 128]
-
-    my_half = pl.multiple_of(core * HALF_ROWS, HALF_ROWS)
-    your_half = pl.multiple_of((1 - core) * HALF_ROWS, HALF_ROWS)
-
     def core_copy(part):
         return pltpu.make_async_remote_copy(
             src_ref=s0.at[part], dst_ref=r0.at[part], send_sem=core_send.at[0, part], recv_sem=core_recv.at[0, part],
             device_id=other_core, device_id_type=MESH,
         )
 
-    def core_back(part):
+    def core_back(part, place):
+        done = fin.at[core, part, place]
         return pltpu.make_async_remote_copy(
-            src_ref=fin.at[core, part], dst_ref=fin.at[core, part], send_sem=core_send.at[1, part],
-            recv_sem=core_recv.at[1, part], device_id=other_core, device_id_type=MESH,
+            src_ref=done, dst_ref=done, send_sem=core_send.at[1, part], recv_sem=core_recv.at[1, part],
+            device_id=other_core, device_id_type=MESH,
         )
+
+    def core_back_waits(part):
+        return all_of(fin.at[1 - core, part], core_send.at[1, part], core_recv.at[1, part])
 
     plane, chunk = ring * ring, HALF_ROWS // (ring * ring)
 
@@ -586,22 +580,30 @@
         a1, a2, _ = ROUTES[part]
         return at[a1] * ring + at[a2]
 
-    def start_copies(back, part):
+    def start_apart(part):
         a1, a2, _ = ROUTES[part]
         for i, j in others:
-            if back:
-                src = dst = fin.at[core, part, spot(part)]
-            else:
-                place = lax.rem(at[a1] + i, ring) * ring + lax.rem(at[a2] + j, ring)
-                src, dst = s1.at[part, place], r1.at[part, i * ring + j]
+            place = lax.rem(at[a1] + i, ring) * ring + lax.rem(at[a2] + j, ring)
             pltpu.make_async_remote_copy(
-                src_ref=src, dst_ref=dst, send_sem=plane_send.at[back, part], recv_sem=plane_recv.at[back, part],
-                device_id=stepped((a1, i), (a2, j)), device_id_type=MESH,
+                src_ref=s1.at[part, place], dst_ref=r1.at[part, i * ring + j], send_sem=plane_send.at[0, part],
+                recv_sem=plane_recv.at[part], device_id=stepped((a1, i), (a2, j)), device_id_type=MESH,
             ).start()
 
-    def plane_waits(back, part):
-        landed = fin.at[core, part, pl.ds(0, plane - 1)] if back else r1.at[part, pl.ds(1, plane - 1)]
-        return all_of(landed, plane_send.at[back, part], plane_recv.at[back, part])
+    def apart_waits(part):
+        return all_of(r1.at[part, pl.ds(1, plane - 1)], plane_send.at[0, part], plane_recv.at[part])
+
+    def back_copy(part, i, j, place):
+        a1, a2, _ = ROUTES[part]
+        return pltpu.make_async_remote_copy(
+            src_ref=fin.at[core, part, place], dst_ref=fin.at[core, part, place], send_sem=plane_send.at[1, part],
+            recv_sem=back_recv.at[part, i * ring + j], device_id=stepped((a1, i), (a2, j)), device_id_type=MESH,
+        )
+
+    def pass_on(part, i, j):
+        a1, a2, _ = ROUTES[part]
+        place = lax.rem(at[a1] - i + ring, ring) * ring + lax.rem(at[a2] - j + ring, ring)
+        back_copy(part, i, j, place).wait_recv()
+        core_back(part, place).start()
 
     def axis_copies(part):
         return [
@@ -609,27 +611,49 @@
                 src_ref=r3.at[part, 0], dst_ref=r3.at[part, step], send_sem=axis_send.at[part, step],
                 recv_sem=axis_recv.at[part, step], device_id=stepped((ROUTES[part][2], step)), device_id_type=MESH,
             )
-            for step in range(1, ring)
+            for step in sorted(range(1, ring), key=lambda step: -min(step, ring - step))
         ]
 
-    def weight_grad(part):
-        for mm in range(3):
-            m = 3 * part + mm
-            rows = col[:, :, 128 * m : 128 * m + 128].reshape(1280, 128)
+    def own_terms(half, part):
+        groups = GROUPS[half][part]
+        count = sum(group < 9 for group in groups)
+        if count:
+            rows = col[:, :, 128 * groups[0] : 128 * (groups[0] + count)].reshape(1280, 128 * count)
             three = contracted(rows, gcat[...].reshape(1280, 384))
-            for o1 in range(3):
-                arf[part, 128 * (3 * o1 + mm) : 128 * (3 * o1 + mm) + 128] = three[:, 128 * o1 : 128 * o1 + 128]
-        s0[part] = arf[part, pl.ds(your_half, HALF_ROWS), :].astype(BF16)
+        for place, group in enumerate(groups):
+            for i in range(3):
+                n = 3 * (group - 9) + i
+                if group < 9:
+                    term = three[128 * place : 128 * place + 128, 128 * i : 128 * i + 128]
+                elif n < 8:
+                    term = contracted(hpart[n // 2], cgx[:, 128 * (n % 2) : 128 * (n % 2) + 128])
+                else:
+                    term = jnp.full((128, 128), misfits, jnp.int32).astype(F32)
+                yield slice(384 * place + 128 * i, 384 * place + 128 * i + 128), term
+
+    def terms_to_send(part):
+        for half in (0, 1):
+            @pl.when(core != half)
+            def _(half=half):
+                for at_rows, term in own_terms(half, part):
+                    s0[part, at_rows] = term.astype(BF16)
         core_copy(part).start()
+
+    def terms_to_keep(part):
+        for half in (0, 1):
+            @pl.when(core == half)
+            def _(half=half):
+                for at_rows, term in own_terms(half, part):
+                    hf[part, at_rows] = term
 
     def start_plane(part):
         core_copy(part).wait_recv()
-        hf[part] = arf[part, pl.ds(my_half, HALF_ROWS), :] + r0[part].astype(F32)
+        hf[part] = hf[part] + r0[part].astype(F32)
         s1[part] = hf[part].astype(BF16).reshape(plane, chunk, 128)
-        start_copies(0, part)
+        start_apart(part)
 
     def start_axis(part):
-        plane_waits(0, part).wait_recv()
+        apart_waits(part).wait_recv()
         mine = hf[part, pl.ds(pl.multiple_of(spot(part) * chunk, chunk), chunk), :]
         for step in range(1, plane):
             mine = mine + r1[part, step].astype(F32)
@@ -646,13 +670,14 @@
             term = r3[part, lax.rem(at[a3] - place + ring, ring)].astype(F32)
             whole = term if whole is None else whole + term
         fin[core, part, spot(part)] = (whole * (1.0 / (nbx * nby))).astype(BF16)
-        start_copies(1, part)
+        for i, j in others:
+            back_copy(part, i, j, spot(part)).start()
+        core_back(part, spot(part)).start()
 
     for part in range(3):
-        for q in ((0, 1), (2,), (3,))[part]:
-            down_grad(q)
-        weight_grad(part)
+        terms_to_send(part)
     for part in range(3):
+        terms_to_keep(part)
         start_plane(part)
     stage_faces(1)
     second_halo = halo_copies(1)
@@ -705,7 +730,7 @@
         copy.wait_send()
     for part in range(3):
         core_copy(part).wait_send()
-        plane_waits(0, part).wait_send()
+        apart_waits(part).wait_send()
         for copy in axis_copies(part):
             copy.wait_send()
 
@@ -713,17 +738,15 @@
     for m in (0, 1):
         coarse_out[m] = rpool[from_row(cfrom[m])]
 
-    for part in range(3):
-        plane_waits(1, part).wait_recv()
-        core_back(part).start()
-    for part in range(3):
-        plane_waits(1, part).wait_send()
-    for part in range(3):
-        core_back(part).wait_recv()
-
+    for i, j in reversed(others):
+        for part in range(3):
+            pass_on(part, i, j)
     row_waits(rsend, c_send, c_recv).wait_send()
     for part in range(3):
-        core_back(part).wait_send()
+        all_of(fin.at[core, part, pl.ds(0, plane - 1)], plane_send.at[1, part], plane_recv.at[part]).wait_send()
+    for part in range(3):
+        core_back_waits(part).wait_recv()
+        core_back_waits(part).wait_send()
 
 
 def finish_kernel(hid, coarse, gfeat, fin, hid_out, coarse_out, gfeat_out, gw_out, gd_out, misfits, gw, gd, sem):
@@ -737,15 +760,23 @@
     leave(coarse, coarse_out)
     leave(gfeat, gfeat_out)
     for part in range(3):
-        low = fin[0, part].reshape(HALF_ROWS, 128).astype(F32).reshape(6, 128, 128)
-        high = fin[1, part].reshape(HALF_ROWS, 128).astype(F32).reshape(6, 128, 128)
-        for o1, three in enumerate((low[:3], low[3:], high[:3])):
-            at = pl.ds(9 * o1 + 3 * part, 3)
-            gw[at] = three
-            leave(gw.at[at], gw_out.at[at])
-        kept = 3 if part < 2 else 2
-        gd[3 * part : 3 * part + kept] = high[3 : 3 + kept]
-        leave(gd.at[pl.ds(3 * part, kept)], gd_out.at[pl.ds(3 * part, kept)])
+        for half in (0, 1):
+            six = fin[half, part].reshape(HALF_ROWS, 128).astype(F32).reshape(6, 128, 128)
+            first, second = GROUPS[half][part]
+            if second < 9:
+                for i in range(3):
+                    gw[9 * i + first] = six[i]
+                    gw[9 * i + second] = six[3 + i]
+                    leave(gw.at[pl.ds(9 * i + first, 2)], gw_out.at[pl.ds(9 * i + first, 2)])
+            elif first < 9:
+                for i in range(3):
+                    gw[9 * i + first] = six[i]
+                    leave(gw.at[9 * i + first], gw_out.at[9 * i + first])
+                gd[0:3] = six[3:]
+                leave(gd.at[pl.ds(0, 3)], gd_out.at[pl.ds(0, 3)])
+            else:
+                gd[3:8] = six[:5]
+                leave(gd.at[pl.ds(3, 5)], gd_out.at[pl.ds(3, 5)])
     count = fin[1, 2].reshape(HALF_ROWS, 128)[640:656].astype(F32)
     misfits[0] = (jnp.max(count) > 0).astype(jnp.int32)
     for copy in copies:
@@ -807,7 +838,6 @@
             pltpu.VMEM((256, 256), BF16),
             pltpu.VMEM((4, 256, 128), F32),
             pltpu.VMEM((20, 64, 384), BF16),
-            pltpu.VMEM((3, PART_ROWS, 128), F32),
             pltpu.VMEM((3, HALF_ROWS, 128), BF16),
             pltpu.VMEM((3, HALF_ROWS, 128), BF16),
             pltpu.VMEM((3, HALF_ROWS, 128), F32),
@@ -821,7 +851,8 @@
             pltpu.SemaphoreType.DMA,
             pltpu.SemaphoreType.DMA,
             pltpu.SemaphoreType.DMA((2, 3)),
-            pltpu.SemaphoreType.DMA((2, 3)),
+            pltpu.SemaphoreType.DMA((3,)),
+            pltpu.SemaphoreType.DMA((3, plane)),
             pltpu.SemaphoreType.DMA((3, nx)),
             pltpu.SemaphoreType.DMA((3, nx)),
             pltpu.SemaphoreType.DMA((2, 3)),
@@ -850,7 +881,7 @@
         scratch_shapes=[
             pltpu.VMEM((27, 128, 128), F32),
             pltpu.VMEM((8, 128, 128), F32),
-            pltpu.SemaphoreType.DMA((15,)),
+            pltpu.SemaphoreType.DMA((20,)),
         ],
         compiler_params=pltpu.CompilerParams(vmem_limit_bytes=16 * 2**20),
     )(hidden, coarse, grad_features, grads)

time: 44.8 us -> 44.4 us (level)
  no operation moved by 1% of the time
where the time goes in v4:
time: 44.4 us; the launch traced here: 44.3 us
  Pallas kernels  42.5 us (96%)
  between operations  0.97 us (2%)
  loops' own time  0.78 us (2%)
    pallas_call x1, Pallas kernels, grid_path(): pl.pallas_call(functools.partial(section_kernel, sizes), out_shape=[jax.S...  40.3 us
    pallas_call x1, Pallas kernels, grid_path(): pl.pallas_call(finish_kernel, out_shape=[jax.ShapeDtypeStruct((2, 8, 64,...  2.24 us

profile of v4, /device:TPU:1, one launch (start us, length us, event | category | flops | bytes accessed | tf_op | source)
XLA Modules:
  0.0 44.3 jit_solution(13367507627048565834)
XLA Ops:
  0.6 0.0 copy-start.36
  0.6 0.0 copy-start.48
  0.7 0.0 copy-start.50
  0.7 0.0 copy-start.52
  0.7 0.0 copy-start.60
  0.7 0.0 copy-start.124
  0.7 0.0 copy-start.126
  0.7 0.0 copy-start.128
  0.7 0.0 copy-start.130
  0.7 40.3 %shard_map.128 = (bf16[2,8,64,128]{3,2,1,0:T(8,128)(2,1)S(1)}, bf16[2,64,128]{2,1,0:T(8,128)(2,1)S(1)}, bf16[2,8,64,128]{3,2,1,0:T(8,128)(2,1)S(1)}, bf16[2,3,16,48,128]{4,3,2,1,0:T(8,128)(2,1)S(1)}) custom-call(s32[2,27]{1,0:T(2,128)} %nb_in.1, s32[2,9]{1,0:T(2,128)} %bitcast.987, s32[2]{0:T(128)} %cdest_in.1, s32[2]{0:T(128)} %cfrom_in.1, ...), custom_call_target="tpu_custom_call" | custom-call | flops 3000000000 | bytes 6000000 | tf_op jit(solution)/shard_map/pallas_call | solution.py:794
  41.0 2.2 %shard_map.129 = (bf16[2,8,64,128]{3,2,1,0:T(8,128)(2,1)}, bf16[2,64,128]{2,1,0:T(8,128)(2,1)}, bf16[2,8,64,128]{3,2,1,0:T(8,128)(2,1)}, f32[27,128,128]{2,1,0:T...) custom-call(bf16[2,8,64,128]{3,2,1,0:T(8,128)(2,1)S(1)} %get-tuple-element.332.hid, ...), custom_call_target="tpu_custom_call" | custom-call | tf_op jit(solution)/shard_map/pallas_call | solution.py:869
  43.3 0.0 copy-done.36
  43.3 0.0 copy-done.48
  43.3 0.0 copy-done.50
  43.3 0.0 copy-done.52
  43.3 0.0 copy-done.60
  43.3 0.0 copy-done.124
  43.3 0.0 copy-done.126
  43.3 0.0 copy-done.128
  43.3 0.0 copy-done.130
  43.4 0.8 %while.49 = (s32[]{:T(128)}, bf16[2,8,8,8,128]{4,3,2,1,0:T(8,128)(2,1)}, bf16[2,64,128]{2,1,0:T(8,128)(2,1)}, bf16[2,8,8,8,128]{4,3,2,1,0:T(8,128)(2,1)}, f32[27...) while((s32[]{:T(128)}, ...), condition=%region_8.11_spmd, body=%region_0.10_spmd | while | flops 2914811392 | bytes 400067200 | solution.py:918
Async XLA Ops:
  0.6 42.6 %copy-start.36 = (bf16[27,128,128]{2,1,0:T(8,128)(2,1)S(1)}, bf16[27,128,128]{2,1,0:T(8,128)(2,1)}, u32[]{:S(2)}) copy-start(bf16[27,128,128]{2,1,0:T(8,128)(2,1)} %weight_in.1) | copy-start | bytes 2654212
  0.6 42.6 %copy-start.48 = (bf16[2,8,8,8,128]{4,3,2,1,0:T(8,128)(2,1)S(1)}, bf16[2,8,8,8,128]{4,3,2,1,0:T(8,128)(2,1)}, u32[]{:S(2)}) copy-start(bf16[2,8,8,8,128]{4,3,2,1,0:T(8,128)(2,1)} %param.27) | copy-start | bytes 786436
  0.7 42.6 %copy-start.50 = (bf16[8,128,128]{2,1,0:T(8,128)(2,1)S(1)}, bf16[8,128,128]{2,1,0:T(8,128)(2,1)}, u32[]{:S(2)}) copy-start(bf16[8,128,128]{2,1,0:T(8,128)(2,1)} %down_in.1) | copy-start | bytes 786436
  0.7 42.6 %copy-start.52 = (bf16[2,8,8,8,128]{4,3,2,1,0:T(8,128)(2,1)S(1)}, bf16[2,8,8,8,128]{4,3,2,1,0:T(8,128)(2,1)}, u32[]{:S(2)}) copy-start(bf16[2,8,8,8,128]{4,3,2,1,0:T(8,128)(2,1)} %param.30) | copy-start | bytes 786436
  0.7 42.6 %copy-start.60 = (bf16[2,64,128]{2,1,0:T(8,128)(2,1)S(1)}, bf16[2,64,128]{2,1,0:T(8,128)(2,1)}, u32[]{:S(2)}) copy-start(bf16[2,64,128]{2,1,0:T(8,128)(2,1)} %gcoarse_in.1) | copy-start | bytes 98308
  0.7 42.6 %copy-start.124 = (s32[2,27]{1,0:T(2,128)S(1)}, s32[2,27]{1,0:T(2,128)}, u32[]{:S(2)}) copy-start(s32[2,27]{1,0:T(2,128)} %nb_in.1) | copy-start | bytes 652
  0.7 42.6 %copy-start.126 = (s32[9,2]{0,1:T(2,128)S(1)}, s32[9,2]{0,1:T(2,128)}, u32[]{:S(2)}) copy-start(s32[9,2]{0,1:T(2,128)} %param.33) | copy-start | bytes 220
  0.7 42.6 %copy-start.128 = (s32[2]{0:T(128)S(1)}, s32[2]{0:T(128)}, u32[]{:S(2)}) copy-start(s32[2]{0:T(128)} %cdest_in.1) | copy-start | bytes 28
  0.7 42.6 %copy-start.130 = (s32[2]{0:T(128)S(1)}, s32[2]{0:T(128)}, u32[]{:S(2)}) copy-start(s32[2]{0:T(128)} %cfrom_in.1) | copy-start | bytes 28
